TPU v7x, 32 devices: a whole 2x2x4 slice. The times are simulated.
32 devices in a mesh: gx: 2 (over y), gy: 4 (over x, core), gz: 4 (over z).
Axes of the slice: x: 2, y: 2, z: 4, core: 2. Of those that a mesh axis runs over, the one named last changes fastest.
Arguments:
- pressure: float32 [32, 64, 512], P('gx', 'gy', 'gz'), may hold values from -6 to 6
- velocity: float32 [3, 32, 64, 512], P(None, 'gx', 'gy', 'gz'), may hold values from -6 to 6
- inv_density: float32 [32, 64, 512], P('gx', 'gy', 'gz'), may hold values from 0.5 to 2
- bulk: float32 [32, 64, 512], P('gx', 'gy', 'gz'), may hold values from 0.25 to 1
- node_weight: float32 [2, 4, 256], P('gx', 'gy'), may hold values from 0.2 to 2
- node_patch: int32 [2, 4, 256], P('gx', 'gy'), may hold values from 0 to 1023, as said below
- patch_slot: int32 [1024], replicated, may hold values from 0 to 1023, as said below
- gauge_x: int32 [256], replicated, may hold values from 0 to 31
- gauge_y: int32 [256], replicated, may hold values from 0 to 63
- gauge_misfit: float32 [4, 256], replicated, may hold values from -6 to 6
Outputs:
- pressure_out: float32 [32, 64, 512], P('gx', 'gy', 'gz')
- velocity_out: float32 [3, 32, 64, 512], P(None, 'gx', 'gy', 'gz')
- slip_grad: float32 [1024], P(('gx', 'gy', 'gz'))
Inputs may be any that keep to these rules, and one draw needn't show every extreme that they name: `node_patch`: of the seafloor nodes of one tile, at most 128 map to patches whose slot lies in one owner's range of 128 slots; in every draw one owner receives exactly 128 from every tile. `patch_slot`: A permutation of the patches.
All inputs are finite; a program needn't handle non-finite values.
Results may differ from a plain program's by a relative error of at most 0.00018.
Values sent between devices are 32-bit elements; how exact they have to be, the bound alone decides.
A program may use at most 64 MiB of HBM per device.

v0:
```python
import jax
import jax.numpy as jnp
from jax import lax
from jax.sharding import PartitionSpec as P

ITERS = 4


time_step = 0.5
margin = 4


def extended(block, sides, width):
    for axis, dim in sides:
        count = lax.axis_size(axis)
        forward = [(i, i + 1) for i in range(count - 1)]
        backward = [(target, source) for source, target in forward]
        low = lax.ppermute(
            lax.slice_in_dim(block, block.shape[dim] - width, None, axis=dim), axis, forward
        )
        high = lax.ppermute(lax.slice_in_dim(block, 0, width, axis=dim), axis, backward)
        block = jnp.concatenate([low, block, high], axis=dim)
    return block


def spread_2(value, axis, source):
    kept = jnp.where(lax.axis_index(axis) == source, value, 0).astype(value.dtype)
    return lax.psum(kept, axis)


def depth_weights(levels, first_crust):
    ocean_last = levels == first_crust - 1
    crust_first = levels == first_crust
    weight_above = jnp.where(ocean_last, 0.5, jnp.where(crust_first, 1.0, 0.5)).astype(jnp.float32)
    weight_here = jnp.where(ocean_last, 0.5, jnp.where(crust_first, -1.5, 0.0)).astype(jnp.float32)
    weight_below = jnp.where(ocean_last, -1.0, jnp.where(crust_first, 0.5, -0.5)).astype(
        jnp.float32
    )
    return (weight_above, weight_here, weight_below)


def source_planes(gauge_x, gauge_y, gauge_misfit, start_x, start_y, span_x, span_y):
    local_x = gauge_x - start_x
    local_y = gauge_y - start_y
    inside = (local_x >= 0) & (local_x < span_x) & (local_y >= 0) & (local_y < span_y)
    gauge_cell = jnp.where(inside, local_x * span_y + local_y, -1)
    gauge_table = (
        gauge_cell[:, None] == jnp.arange(span_x * span_y, dtype=jnp.int32)[None, :]
    ).astype(jnp.float32)
    return jnp.dot(gauge_misfit, gauge_table, precision=lax.Precision.HIGHEST).reshape(
        gauge_misfit.shape[0], span_x, span_y
    )


def local_step(pressure, velocity, inv_density, bulk, weights, source_plane, top_mask):
    weight_above, weight_here, weight_below = weights
    padded = jnp.pad(pressure, 1)
    slope_x = 0.5 * (padded[2:, 1:-1, 1:-1] - padded[:-2, 1:-1, 1:-1])
    slope_y = 0.5 * (padded[1:-1, 2:, 1:-1] - padded[1:-1, :-2, 1:-1])
    slope_z = (
        weight_above * padded[1:-1, 1:-1, 2:]
        + weight_here * pressure
        + weight_below * padded[1:-1, 1:-1, :-2]
    )
    velocity = jnp.stack(
        [
            velocity[0] - time_step * inv_density * slope_x,
            velocity[1] - time_step * inv_density * slope_y,
            velocity[2] - time_step * inv_density * slope_z,
        ]
    )
    along_x = jnp.pad(velocity[0], ((1, 1), (0, 0), (0, 0)))
    along_y = jnp.pad(velocity[1], ((0, 0), (1, 1), (0, 0)))
    along_z = jnp.pad(velocity[2], ((0, 0), (0, 0), (1, 1)))
    spread = (
        0.5 * (along_x[2:] - along_x[:-2])
        + 0.5 * (along_y[:, 2:] - along_y[:, :-2])
        + (
            weight_above * along_z[:, :, 2:]
            + weight_here * velocity[2]
            + weight_below * along_z[:, :, :-2]
        )
    )
    pressure = pressure - time_step * bulk * spread
    pressure = pressure + time_step * source_plane[:, :, None] * top_mask[None, None, :]
    return (pressure, velocity)


def local(
    pressure,
    velocity,
    inv_density,
    bulk,
    node_weight,
    node_patch,
    patch_slot,
    gauge_x,
    gauge_y,
    gauge_misfit,
):
    rows_x, rows_y, depth = pressure.shape
    tiles_z = lax.axis_size("gz")
    depth_index = lax.axis_index("gz")
    first_crust = tiles_z // 2 * depth
    seafloor = jnp.zeros((rows_x, rows_y), jnp.float32)
    levels = depth_index * depth - margin + jnp.arange(depth + 2 * margin, dtype=jnp.int32)
    weights = depth_weights(levels, first_crust)
    top_mask = (levels == 0).astype(jnp.float32)
    sources = source_planes(
        gauge_x,
        gauge_y,
        gauge_misfit,
        lax.axis_index("gx") * rows_x - margin,
        lax.axis_index("gy") * rows_y - margin,
        rows_x + 2 * margin,
        rows_y + 2 * margin,
    )
    media = extended(jnp.stack([inv_density, bulk]), (("gx", 1), ("gy", 2), ("gz", 3)), margin)
    fields = jnp.concatenate([pressure[None], velocity], axis=0)
    for group in range(ITERS // 2):
        wide = extended(fields, (("gx", 1), ("gy", 2), ("gz", 3)), margin)
        wide_pressure = wide[0]
        wide_velocity = wide[1:]
        for inner in range(2):
            instant = 2 * group + inner
            seafloor = seafloor + 0.5 * (
                wide_pressure[margin:-margin, margin:-margin, margin - 1]
                + wide_pressure[margin:-margin, margin:-margin, margin]
            )
            wide_pressure, wide_velocity = local_step(
                wide_pressure,
                wide_velocity,
                media[0],
                media[1],
                weights,
                sources[instant],
                top_mask,
            )
        fields = jnp.concatenate([wide_pressure[None], wide_velocity], axis=0)[
            :, margin:-margin, margin:-margin, margin:-margin
        ]
    pressure = fields[0]
    velocity = fields[1:]
    sea_count = rows_x * rows_y
    owners_count = lax.axis_size("gx") * lax.axis_size("gy")
    patch_count = patch_slot.shape[0] // owners_count
    piece_count = patch_count // tiles_z
    root_tile = tiles_z // 2
    sea_values = node_weight[0, 0] * seafloor.reshape(sea_count)
    sea_values = spread_2(sea_values, "gz", root_tile)
    slots = patch_slot[node_patch[0, 0]]
    capacity = 4 * sea_count // owners_count
    owners = slots // patch_count
    within = slots % patch_count
    order = jnp.argsort(owners, stable=True)
    sorted_owner = owners[order]
    counts = jnp.sum(
        (owners[:, None] == jnp.arange(owners_count, dtype=jnp.int32)[None, :]).astype(jnp.int32),
        axis=0,
    )
    starts = jnp.cumsum(counts) - counts
    ranks = jnp.arange(sea_count, dtype=jnp.int32) - starts[sorted_owner]
    target = sorted_owner * capacity + ranks
    send_values = (
        jnp.zeros((owners_count * capacity,), jnp.float32)
        .at[target]
        .set(sea_values[order])
        .reshape(owners_count, capacity)
    )
    send_ids = (
        jnp.zeros((owners_count * capacity,), jnp.int32)
        .at[target]
        .set(within[order])
        .reshape(owners_count, capacity)
    )
    got_values, got_ids = (
        lax.all_to_all(send_values, ("gx", "gy"), split_axis=0, concat_axis=0, tiled=True),
        lax.all_to_all(send_ids, ("gx", "gy"), split_axis=0, concat_axis=0, tiled=True),
    )
    matches = got_ids.reshape(-1)[:, None] == jnp.arange(patch_count, dtype=jnp.int32)[None, :]
    slip_grad = jnp.sum(jnp.where(matches, got_values.reshape(-1)[:, None], 0.0), axis=0)
    slip_grad = lax.dynamic_slice_in_dim(slip_grad, depth_index * piece_count, piece_count)
    return (pressure, velocity, slip_grad)


def solution(mesh):
    placed = (
        P("gx", "gy", "gz"),
        P(None, "gx", "gy", "gz"),
        P("gx", "gy", "gz"),
        P("gx", "gy", "gz"),
        P("gx", "gy", None),
        P("gx", "gy", None),
        P(),
        P(),
        P(),
        P(),
    )
    return jax.shard_map(
        local,
        mesh=mesh,
        in_specs=placed,
        out_specs=(P("gx", "gy", "gz"), P(None, "gx", "gy", "gz"), P(("gx", "gy", "gz"))),
        check_vma=False,
    )
```

profile of v0, /device:TPU:0, one launch (start us, length us, event | category | flops | bytes accessed | tf_op | source)
XLA Modules:
  0.0 216.5 jit_solution(1949481563588804365)
XLA Ops:
  1.5 4.9 %collective-permute-start.6 = (f32[2,4,16,128]{3,2,1,0:T(8,128)S(1)}, f32[2,4,16,128]{3,2,1,0:T(8,128)S(1)}, u32[]{:S(2)}, u32[]{:S(2)}) collective-permute-start(f32[2,4,16,128]{3,2,1,0:T(8,128)S(1)} %get-tuple-element.40), channel_id=1, source_target_pairs={{0,16},{1,17},{2,18},{3,19},{4,20},{5,21},{6,22},{7,23},{8,24},{9,... | collective-permute-start | bytes 196616 | tf_op jit(solution)/shard_map/ppermute | solution.py:18
  8.7 4.6 %collective-permute-start = (f32[4,4,16,128]{3,2,1,0:T(8,128)S(1)}, f32[4,4,16,128]{3,2,1,0:T(8,128)S(1)}, u32[]{:S(2)}, u32[]{:S(2)}) collective-permute-start(f32[4,4,16,128]{3,2,1,0:T(8,128)S(1)} %get-tuple-element.36), channel_id=1, source_target_pairs={{0,16},{1,17},{2,18},{3,19},{4,20},{5,21},{6,22},{7,23},{8,24},{9,... | collective-permute-start | bytes 393224 | tf_op jit(solution)/shard_map/ppermute | solution.py:18
  19.1 3.2 %sort.17 = (s32[256]{0:T(256)}, s32[256]{0:T(256)S(1)}) sort(s32[256]{0:T(256)S(1)} %get-tuple-element.43, s32[256]{0:T(256)S(1)} %iota.32), dimensions={0}, to_apply=%region_0.1 | sort | flops 2048 | bytes 4096 | tf_op jit(solution)/shard_map/jit(argsort)/sort | solution.py:155
  31.0 4.8 %collective-permute-start.2 = (f32[4,24,4,128]{3,1,2,0:T(8,128)}, f32[4,24,4,128]{3,1,2,0:T(8,128)S(1)}, u32[]{:S(2)}, u32[]{:S(2)}) collective-permute-start(f32[4,24,4,128]{3,1,2,0:T(8,128)} %copy.67), channel_id=1, source_target_pairs={{0,4},{4,8},{8,12},{1,5},{5,9},{9,13},{2,6},{6,10},{10,14},{3,7},{... | collective-permute-start | bytes 589832 | tf_op jit(solution)/shard_map/ppermute | solution.py:18
  42.3 5.4 %pad_maximum_fusion.2 = f32[2,24,24,128]{2,1,3,0:T(8,128)S(1)} fusion(f32[2,24,4,128]{2,1,3,0:T(8,128)} %copy.55, f32[2,24,16,128]{2,1,3,0:T(8,128)} %copy.54, f32[2,24,4,128]{2,1,3,0:T(8,128)} %copy.53), kind=kLoop, calls=%fused_computation.8 | loop fusion | flops 294912 | bytes 1179648 | tf_op jit(solution)/shard_map/concatenate | solution.py:22
  48.4 4.1 %collective-permute-start.10 = (f32[2,24,24,4]{2,1,3,0:T(8,128)}, f32[2,24,24,4]{2,1,3,0:T(8,128)}, u32[]{:S(2)}, u32[]{:S(2)}) collective-permute-start(f32[2,24,24,4]{2,1,3,0:T(8,128)} %get-tuple-element.22), channel_id=1, source_target_pairs={{0,1},{1,2},{2,3},{4,5},{5,6},{6,7},{8,9},{9,10},{10,11},{12,13},{... | collective-permute-start | bytes 55304 | tf_op jit(solution)/shard_map/ppermute | solution.py:18
  59.7 5.0 %copy.46 = f32[4,24,16,128]{2,1,3,0:T(8,128)} copy(f32[4,24,16,128]{3,2,1,0:T(8,128)} %copy-done.4) | data formatting | bytes 1572864 | tf_op jit(solution)/shard_map/concatenate | solution.py:22
  69.1 4.3 %copy.45 = f32[4,24,4,128]{2,1,3,0:T(8,128)} copy(f32[4,24,4,128]{3,1,2,0:T(8,128)S(1)} %collective-permute-done.2) | data formatting | bytes 393216 | tf_op jit(solution)/shard_map/ppermute | solution.py:18
  73.3 4.3 %copy.47 = f32[4,24,4,128]{2,1,3,0:T(8,128)} copy(f32[4,24,4,128]{3,1,2,0:T(8,128)S(1)} %collective-permute-done.3) | data formatting | bytes 393216 | tf_op jit(solution)/shard_map/ppermute | solution.py:21
  77.7 8.2 %pad_maximum_fusion = f32[4,24,24,128]{2,1,3,0:T(8,128)S(1)} fusion(f32[4,24,4,128]{2,1,3,0:T(8,128)} %copy.47, f32[4,24,16,128]{2,1,3,0:T(8,128)} %copy.46, f32[4,24,4,128]{2,1,3,0:T(8,128)} %copy.45), kind=kLoop, calls=%fused_computation.6 | loop fusion | flops 589824 | bytes 2359296 | tf_op jit(solution)/shard_map/concatenate | solution.py:22
  86.7 5.2 %collective-permute-start.4 = (f32[4,24,24,4]{2,1,3,0:T(8,128)S(1)}, f32[4,24,24,4]{2,1,3,0:T(8,128)}, u32[]{:S(2)}, u32[]{:S(2)}) collective-permute-start(f32[4,24,24,4]{2,1,3,0:T(8,128)S(1)} %get-tuple-element.14), channel_id=1, source_target_pairs={{0,1},{1,2},{2,3},{4,5},{5,6},{6,7},{8,9},{9,10},{10,11},{12,13},{... | collective-permute-start | bytes 110600 | tf_op jit(solution)/shard_map/ppermute | solution.py:18
  93.9 4.4 %copy.49 = f32[4,24,24,128]{3,2,1,0:T(8,128)S(1)} copy(f32[4,24,24,128]{2,1,3,0:T(8,128)} %copy-done.3) | data formatting | bytes 2359296 | tf_op jit(solution)/shard_map/concatenate | solution.py:22
  109.3 4.6 %collective-permute-start.12 = (f32[4,4,16,128]{3,2,1,0:T(8,128)S(1)}, f32[4,4,16,128]{3,2,1,0:T(8,128)S(1)}, u32[]{:S(2)}, u32[]{:S(2)}) collective-permute-start(f32[4,4,16,128]{3,2,1,0:T(8,128)S(1)} %get-tuple-element.24), channel_id=1, source_target_pairs={{0,16},{1,17},{2,18},{3,19},{4,20},{5,21},{6,22},{7,23},{8,24},{9,... | collective-permute-start | bytes 393224 | tf_op jit(solution)/shard_map/ppermute | solution.py:18
  115.2 4.4 %compare_select_fusion.3 = s32[256,1]{0,1:T(1,128)S(1)} fusion(s32[]{:T(128)} %bitcast.29, s32[]{:T(128)} %bitcast.30, s32[]{:T(128)} %bitcast.31, s32[]{:T(128)} %bitcast.32, s32[]{:T(128)} %bitcast.33, s32[]{:T(128)} %bitcast.35, s32[]{:T(128)} %bitcast.34, s32[256,1]{0,1:T(1,128)S(1)} %bitcast.125), kind=kLoop, calls=%fused_computation.197 | loop fusion | flops 3840 | bytes 2076 | tf_op jit(solution)/shard_map/gather | solution.py:162
  126.7 4.1 %copy.62 = f32[4,24,16,128]{2,1,3,0:T(8,128)} copy(f32[4,24,16,128]{3,2,1,0:T(8,128)S(1)} %fusion.1) | data formatting | bytes 1572864 | tf_op jit(solution)/shard_map/concatenate | solution.py:22
  130.8 4.2 %copy.61 = f32[4,24,4,128]{2,1,3,0:T(8,128)} copy(f32[4,24,4,128]{3,1,2,0:T(8,128)S(1)} %collective-permute-done.14) | data formatting | bytes 393216 | tf_op jit(solution)/shard_map/ppermute | solution.py:18
  135.0 4.3 %copy.63 = f32[4,24,4,128]{2,1,3,0:T(8,128)} copy(f32[4,24,4,128]{3,1,2,0:T(8,128)S(1)} %collective-permute-done.15) | data formatting | bytes 393216 | tf_op jit(solution)/shard_map/ppermute | solution.py:21
  139.3 8.2 %pad_maximum_fusion.1 = f32[4,24,24,128]{2,1,3,0:T(8,128)S(1)} fusion(f32[4,24,4,128]{2,1,3,0:T(8,128)} %copy.63, f32[4,24,16,128]{2,1,3,0:T(8,128)} %copy.62, f32[4,24,4,128]{2,1,3,0:T(8,128)} %copy.61), kind=kLoop, calls=%fused_computation.7 | loop fusion | flops 589824 | bytes 2359296 | tf_op jit(solution)/shard_map/concatenate | solution.py:22
  150.9 5.3 %collective-permute-start.16 = (f32[4,24,24,4]{2,1,3,0:T(8,128)}, f32[4,24,24,4]{2,1,3,0:T(8,128)}, u32[]{:S(2)}, u32[]{:S(2)}) collective-permute-start(f32[4,24,24,4]{2,1,3,0:T(8,128)} %get-tuple-element.12), channel_id=1, source_target_pairs={{0,1},{1,2},{2,3},{4,5},{5,6},{6,7},{8,9},{9,10},{10,11},{12,13},{... | collective-permute-start | bytes 110600 | tf_op jit(solution)/shard_map/ppermute | solution.py:18
  161.6 7.1 %all-to-all-start = ((s32[8,1,128]{2,1,0:T(1,128)}), s32[8,1,128]{2,1,0:T(1,128)}, u32[]{:S(2)}, u32[]{:S(2)}) async-start(s32[8,1,128]{2,1,0:T(1,128)} %bitcast.39), calls=%async_computation | async-start | bytes 8192 | tf_op jit(solution)/shard_map/all_to_all | solution.py:178
  170.1 4.3 %copy.65 = f32[4,24,24,128]{3,2,1,0:T(8,128)S(1)} copy(f32[4,24,24,128]{2,1,3,0:T(8,128)} %copy-done.2) | data formatting | bytes 2359296 | tf_op jit(solution)/shard_map/concatenate | solution.py:22
  188.9 12.9 %psum.7 = f32[256]{0:T(256)S(1)} all-reduce(f32[256]{0:T(256)S(1)} %multiply_select_fusion), channel_id=1, replica_groups=mesh['gx'=2,'gy'=4,'gz'=4] {'gz'}, use_global_device_ids=true, to_apply=%region_4.5 | all-reduce | flops 256 | bytes 2048 | tf_op jit(solution)/shard_map/psum | solution.py:28
  206.0 4.2 %all-to-all-start.1 = ((f32[8,1,128]{2,1,0:T(1,128)}), f32[8,1,128]{2,1,0:T(1,128)S(1)}, u32[]{:S(2)}, u32[]{:S(2)}) async-start(f32[8,1,128]{2,1,0:T(1,128)} %bitcast.42), calls=%async_computation.1 | async-start | bytes 8192 | tf_op jit(solution)/shard_map/all_to_all | solution.py:177
  211.1 3.7 %all-to-all-done.1 = f32[8,1,128]{2,1,0:T(1,128)S(1)} async-done(((f32[8,1,128]{2,1,0:T(1,128)}), f32[8,1,128]{2,1,0:T(1,128)S(1)}, u32[]{:S(2)}, u32[]{:S(2)}) %all-to-all-start.1) | async-done | bytes 4128 | tf_op jit(solution)/shard_map/all_to_all | solution.py:177
  (155 shorter events, 89.7 us)
Async XLA Ops:
  0.6 23.7 %copy-start.8 = (f32[16,16,128]{2,1,0:T(8,128)S(1)}, f32[16,16,128]{2,1,0:T(8,128)}, u32[]{:S(2)}) copy-start(f32[16,16,128]{2,1,0:T(8,128)} %param.12) | copy-start | bytes 393220
  1.5 22.8 %collective-permute-start.6 = (f32[2,4,16,128]{3,2,1,0:T(8,128)S(1)}, f32[2,4,16,128]{3,2,1,0:T(8,128)S(1)}, u32[]{:S(2)}, u32[]{:S(2)}) collective-permute-start(f32[2,4,16,128]{3,2,1,0:T(8,128)S(1)} %get-tuple-element.40), channel_id=1, source_target_pairs={{0,16},{1,17},{2,18},{3,19},{4,20},{5,21},{6,22},{7,23},{8,24},{9,... | collective-permute-start | bytes 196616 | tf_op jit(solution)/shard_map/ppermute | solution.py:18
  6.4 17.9 %collective-permute-start.7 = (f32[2,4,16,128]{3,2,1,0:T(8,128)S(1)}, f32[2,4,16,128]{3,2,1,0:T(8,128)S(1)}, u32[]{:S(2)}, u32[]{:S(2)}) collective-permute-start(f32[2,4,16,128]{3,2,1,0:T(8,128)S(1)} %get-tuple-element.41), channel_id=1, source_target_pairs={{16,0},{17,1},{18,2},{19,3},{20,4},{21,5},{22,6},{23,7},{24,8},{25... | collective-permute-start | bytes 196616 | tf_op jit(solution)/shard_map/ppermute | solution.py:21
  8.7 20.5 %collective-permute-start = (f32[4,4,16,128]{3,2,1,0:T(8,128)S(1)}, f32[4,4,16,128]{3,2,1,0:T(8,128)S(1)}, u32[]{:S(2)}, u32[]{:S(2)}) collective-permute-start(f32[4,4,16,128]{3,2,1,0:T(8,128)S(1)} %get-tuple-element.36), channel_id=1, source_target_pairs={{0,16},{1,17},{2,18},{3,19},{4,20},{5,21},{6,22},{7,23},{8,24},{9,... | collective-permute-start | bytes 393224 | tf_op jit(solution)/shard_map/ppermute | solution.py:18
  13.2 16.0 %collective-permute-start.1 = (f32[4,4,16,128]{3,2,1,0:T(8,128)S(1)}, f32[4,4,16,128]{3,2,1,0:T(8,128)S(1)}, u32[]{:S(2)}, u32[]{:S(2)}) collective-permute-start(f32[4,4,16,128]{3,2,1,0:T(8,128)S(1)} %get-tuple-element.37), channel_id=1, source_target_pairs={{16,0},{17,1},{18,2},{19,3},{20,4},{21,5},{22,6},{23,7},{24,8},{25... | collective-permute-start | bytes 393224 | tf_op jit(solution)/shard_map/ppermute | solution.py:21
  26.6 11.1 %collective-permute-start.8 = (f32[2,24,4,128]{3,1,2,0:T(8,128)S(1)}, f32[2,24,4,128]{3,1,2,0:T(8,128)S(1)}, u32[]{:S(2)}, u32[]{:S(2)}) collective-permute-start(f32[2,24,4,128]{3,1,2,0:T(8,128)S(1)} %copy.69), channel_id=1, source_target_pairs={{0,4},{4,8},{8,12},{1,5},{5,9},{9,13},{2,6},{6,10},{10,14},{3,7},{... | collective-permute-start | bytes 294920 | tf_op jit(solution)/shard_map/ppermute | solution.py:18
  27.9 12.1 %collective-permute-start.9 = (f32[2,24,4,128]{3,1,2,0:T(8,128)S(1)}, f32[2,24,4,128]{3,1,2,0:T(8,128)S(1)}, u32[]{:S(2)}, u32[]{:S(2)}) collective-permute-start(f32[2,24,4,128]{3,1,2,0:T(8,128)S(1)} %copy.70), channel_id=1, source_target_pairs={{4,0},{8,4},{12,8},{5,1},{9,5},{13,9},{6,2},{10,6},{14,10},{7,3},{... | collective-permute-start | bytes 294920 | tf_op jit(solution)/shard_map/ppermute | solution.py:21
  31.0 38.1 %collective-permute-start.2 = (f32[4,24,4,128]{3,1,2,0:T(8,128)}, f32[4,24,4,128]{3,1,2,0:T(8,128)S(1)}, u32[]{:S(2)}, u32[]{:S(2)}) collective-permute-start(f32[4,24,4,128]{3,1,2,0:T(8,128)} %copy.67), channel_id=1, source_target_pairs={{0,4},{4,8},{8,12},{1,5},{5,9},{9,13},{2,6},{6,10},{10,14},{3,7},{... | collective-permute-start | bytes 589832 | tf_op jit(solution)/shard_map/ppermute | solution.py:18
  36.4 36.9 %collective-permute-start.3 = (f32[4,24,4,128]{3,1,2,0:T(8,128)}, f32[4,24,4,128]{3,1,2,0:T(8,128)S(1)}, u32[]{:S(2)}, u32[]{:S(2)}) collective-permute-start(f32[4,24,4,128]{3,1,2,0:T(8,128)} %copy.68), channel_id=1, source_target_pairs={{4,0},{8,4},{12,8},{5,1},{9,5},{13,9},{6,2},{10,6},{14,10},{7,3},{... | collective-permute-start | bytes 589832 | tf_op jit(solution)/shard_map/ppermute | solution.py:21
  48.4 18.2 %collective-permute-start.10 = (f32[2,24,24,4]{2,1,3,0:T(8,128)}, f32[2,24,24,4]{2,1,3,0:T(8,128)}, u32[]{:S(2)}, u32[]{:S(2)}) collective-permute-start(f32[2,24,24,4]{2,1,3,0:T(8,128)} %get-tuple-element.22), channel_id=1, source_target_pairs={{0,1},{1,2},{2,3},{4,5},{5,6},{6,7},{8,9},{9,10},{10,11},{12,13},{... | collective-permute-start | bytes 55304 | tf_op jit(solution)/shard_map/ppermute | solution.py:18
  52.5 15.3 %collective-permute-start.11 = (f32[2,24,24,4]{2,1,3,0:T(8,128)}, f32[2,24,24,4]{2,1,3,0:T(8,128)}, u32[]{:S(2)}, u32[]{:S(2)}) collective-permute-start(f32[2,24,24,4]{2,1,3,0:T(8,128)} %get-tuple-element.23), channel_id=1, source_target_pairs={{1,0},{2,1},{3,2},{5,4},{6,5},{7,6},{9,8},{10,9},{11,10},{13,12},{... | collective-permute-start | bytes 55304 | tf_op jit(solution)/shard_map/ppermute | solution.py:21
  86.7 11.6 %collective-permute-start.4 = (f32[4,24,24,4]{2,1,3,0:T(8,128)S(1)}, f32[4,24,24,4]{2,1,3,0:T(8,128)}, u32[]{:S(2)}, u32[]{:S(2)}) collective-permute-start(f32[4,24,24,4]{2,1,3,0:T(8,128)S(1)} %get-tuple-element.14), channel_id=1, source_target_pairs={{0,1},{1,2},{2,3},{4,5},{5,6},{6,7},{8,9},{9,10},{10,11},{12,13},{... | collective-permute-start | bytes 110600 | tf_op jit(solution)/shard_map/ppermute | solution.py:18
  91.9 9.5 %collective-permute-start.5 = (f32[4,24,24,4]{2,1,3,0:T(8,128)}, f32[4,24,24,4]{2,1,3,0:T(8,128)}, u32[]{:S(2)}, u32[]{:S(2)}) collective-permute-start(f32[4,24,24,4]{2,1,3,0:T(8,128)} %get-tuple-element.15), channel_id=1, source_target_pairs={{1,0},{2,1},{3,2},{5,4},{6,5},{7,6},{9,8},{10,9},{11,10},{13,12},{... | collective-permute-start | bytes 110600 | tf_op jit(solution)/shard_map/ppermute | solution.py:21
  109.3 10.3 %collective-permute-start.12 = (f32[4,4,16,128]{3,2,1,0:T(8,128)S(1)}, f32[4,4,16,128]{3,2,1,0:T(8,128)S(1)}, u32[]{:S(2)}, u32[]{:S(2)}) collective-permute-start(f32[4,4,16,128]{3,2,1,0:T(8,128)S(1)} %get-tuple-element.24), channel_id=1, source_target_pairs={{0,16},{1,17},{2,18},{3,19},{4,20},{5,21},{6,22},{7,23},{8,24},{9,... | collective-permute-start | bytes 393224 | tf_op jit(solution)/shard_map/ppermute | solution.py:18
  113.9 7.3 %collective-permute-start.13 = (f32[4,4,16,128]{3,2,1,0:T(8,128)S(1)}, f32[4,4,16,128]{3,2,1,0:T(8,128)S(1)}, u32[]{:S(2)}, u32[]{:S(2)}) collective-permute-start(f32[4,4,16,128]{3,2,1,0:T(8,128)S(1)} %get-tuple-element.25), channel_id=1, source_target_pairs={{16,0},{17,1},{18,2},{19,3},{20,4},{21,5},{22,6},{23,7},{24,8},{25... | collective-permute-start | bytes 393224 | tf_op jit(solution)/shard_map/ppermute | solution.py:21
  122.2 8.6 %collective-permute-start.14 = (f32[4,24,4,128]{3,1,2,0:T(8,128)}, f32[4,24,4,128]{3,1,2,0:T(8,128)S(1)}, u32[]{:S(2)}, u32[]{:S(2)}) collective-permute-start(f32[4,24,4,128]{3,1,2,0:T(8,128)} %copy.71), channel_id=1, source_target_pairs={{0,4},{4,8},{8,12},{1,5},{5,9},{9,13},{2,6},{6,10},{10,14},{3,7},{... | collective-permute-start | bytes 589832 | tf_op jit(solution)/shard_map/ppermute | solution.py:18
  124.2 10.8 %collective-permute-start.15 = (f32[4,24,4,128]{3,1,2,0:T(8,128)}, f32[4,24,4,128]{3,1,2,0:T(8,128)S(1)}, u32[]{:S(2)}, u32[]{:S(2)}) collective-permute-start(f32[4,24,4,128]{3,1,2,0:T(8,128)} %copy.72), channel_id=1, source_target_pairs={{4,0},{8,4},{12,8},{5,1},{9,5},{13,9},{6,2},{10,6},{14,10},{7,3},{... | collective-permute-start | bytes 589832 | tf_op jit(solution)/shard_map/ppermute | solution.py:21
  139.3 29.4 %copy-start.17 = (f32[576]{0:T(1024)S(1)}, f32[576]{0:T(1024)}, u32[]{:S(2)}) copy-start(f32[576]{0:T(1024)} %get-tuple-element.9) | copy-start | bytes 6916
  139.3 30.1 %copy-start.16 = (f32[576]{0:T(1024)S(1)}, f32[576]{0:T(1024)}, u32[]{:S(2)}) copy-start(f32[576]{0:T(1024)} %get-tuple-element.8) | copy-start | bytes 6916
  150.9 23.5 %collective-permute-start.16 = (f32[4,24,24,4]{2,1,3,0:T(8,128)}, f32[4,24,24,4]{2,1,3,0:T(8,128)}, u32[]{:S(2)}, u32[]{:S(2)}) collective-permute-start(f32[4,24,24,4]{2,1,3,0:T(8,128)} %get-tuple-element.12), channel_id=1, source_target_pairs={{0,1},{1,2},{2,3},{4,5},{5,6},{6,7},{8,9},{9,10},{10,11},{12,13},{... | collective-permute-start | bytes 110600 | tf_op jit(solution)/shard_map/ppermute | solution.py:18
  156.3 20.8 %collective-permute-start.17 = (f32[4,24,24,4]{2,1,3,0:T(8,128)}, f32[4,24,24,4]{2,1,3,0:T(8,128)}, u32[]{:S(2)}, u32[]{:S(2)}) collective-permute-start(f32[4,24,24,4]{2,1,3,0:T(8,128)} %get-tuple-element.13), channel_id=1, source_target_pairs={{1,0},{2,1},{3,2},{5,4},{6,5},{7,6},{9,8},{10,9},{11,10},{13,12},{... | collective-permute-start | bytes 110600 | tf_op jit(solution)/shard_map/ppermute | solution.py:21
  161.6 44.3 %all-to-all-start = ((s32[8,1,128]{2,1,0:T(1,128)}), s32[8,1,128]{2,1,0:T(1,128)}, u32[]{:S(2)}, u32[]{:S(2)}) async-start(s32[8,1,128]{2,1,0:T(1,128)} %bitcast.39), calls=%async_computation | async-start | bytes 8192 | tf_op jit(solution)/shard_map/all_to_all | solution.py:178
  186.7 29.8 %copy-start.1 = (f32[4,256]{1,0:T(4,128)S(1)}, f32[4,256]{1,0:T(4,128)}, u32[]{:S(2)}) copy-start(f32[4,256]{1,0:T(4,128)} %param.19) | copy-start | bytes 12292
  206.0 8.9 %all-to-all-start.1 = ((f32[8,1,128]{2,1,0:T(1,128)}), f32[8,1,128]{2,1,0:T(1,128)S(1)}, u32[]{:S(2)}, u32[]{:S(2)}) async-start(f32[8,1,128]{2,1,0:T(1,128)} %bitcast.42), calls=%async_computation.1 | async-start | bytes 8192 | tf_op jit(solution)/shard_map/all_to_all | solution.py:177
  (20 other events, 139.3 us)
where the time goes:
time: 218 us; the launch traced here: 216 us
  local copies, waits for them, and re-layouts  84.7 us (39%)
  starting transfers between devices  59 us (27%)
  other arithmetic  51.4 us (24%)
  blocking collectives  12.9 us (6%)
  waiting for transfers between devices  6.94 us (3%)
    ppermute x9, starting transfers between devices, extended(): lax.ppermute(lax.slice_in_dim(block, block.shape[dim] - width, None, axis...  36 us
    concatenate x9, other arithmetic, extended(): block = jnp.concatenate([low, block, high], axis=dim)  27.5 us
    concatenate x6, local copies, waits for them, and re-layouts, extended(): block = jnp.concatenate([low, block, high], axis=dim)  21.8 us
    ppermute x6, local copies, waits for them, and re-layouts, extended(): lax.ppermute(lax.slice_in_dim(block, 0, width, axis=dim), axis, backward)  17.3 us
    ppermute x6, local copies, waits for them, and re-layouts, extended(): lax.ppermute(lax.slice_in_dim(block, block.shape[dim] - width, None, axis...  16.2 us
    psum x1, blocking collectives, spread_2(): return lax.psum(kept, axis)  12.9 us
    ppermute x9, starting transfers between devices, extended(): lax.ppermute(lax.slice_in_dim(block, 0, width, axis=dim), axis, backward)  11.7 us
    all_to_all x1, starting transfers between devices, local(): lax.all_to_all(send_ids, ('gx', 'gy'), split_axis=0, concat_axis=0, tiled...  7.07 us
  transfers between devices with their start and end apart: 20, of which 3 were waited for; matrix products, arithmetic and copies ran while one was open for 44% of the time, Pallas kernels for 0%

commit v1 on v0

v1 whole, which is shorter than its diff:
```python
import functools

import jax
import jax.numpy as jnp
from jax import lax
from jax.experimental import pallas as pl
from jax.experimental.pallas import tpu as pltpu
from jax.sharding import PartitionSpec as P

ITERS = 4
MESH_ID = pl.DeviceIdType.MESH
AXES = ("gx", "gy", "gz")
YA = 8
F32 = jnp.float32
HIGHEST = lax.Precision.HIGHEST
NT = (((1,), (1,)), ((), ()))


def kernel(
    sizes,
    p_in,
    v_in,
    d_in,
    b_in,
    weight_ref,
    patch_ref,
    slot_ref,
    gx_ref,
    gy_ref,
    misfit_ref,
    p_out,
    v_out,
    slip_out,
    p_ext,
    vx,
    vy,
    vz,
    inv,
    inv_y,
    bulk,
    pack_edge,
    vz_edge,
    fill_p,
    fill_v,
    y_send,
    y_recv,
    z_send,
    z_recv,
    yi_send,
    yi_recv,
    zi_send,
    zi_recv,
    source,
    slot_hot,
    spread_hot,
    part,
    got,
    load_sem,
    store_sem,
    send_sem,
    recv_sem,
    init_send,
    init_recv,
    slip_send,
    slip_recv,
):
    n_x, n_y, n_z = sizes
    rows_x, rows_y, depth = p_in.shape
    cells = rows_x * rows_y
    halves = rows_y // 8
    me = [lax.axis_index(a) for a in AXES]
    tiles = n_x * n_y
    tile = me[0] * n_y + me[1]
    root = n_z // 2
    has = {}
    other = {}
    for a in range(3):
        has[a, 0] = me[a] > 0
        has[a, 1] = me[a] < sizes[a] - 1
        for side in (0, 1):
            to = list(me)
            to[a] = me[a] + (2 * side - 1)
            other[a, side] = tuple(to)
    faces = [(a, side) for a in range(3) for side in (0, 1) if sizes[a] > 1]

    y_in = pl.ds(YA, rows_y)
    x_in = pl.ds(2, rows_x)
    loads = [
        pltpu.make_async_copy(p_in, p_ext.at[0, x_in, y_in], load_sem.at[0]),
        pltpu.make_async_copy(d_in, inv.at[pl.ds(1, rows_x)], load_sem.at[1]),
        pltpu.make_async_copy(v_in.at[2], vz, load_sem.at[2]),
        pltpu.make_async_copy(v_in.at[1], vy.at[:, y_in], load_sem.at[3]),
        pltpu.make_async_copy(v_in.at[0], vx.at[pl.ds(1, rows_x)], load_sem.at[4]),
        pltpu.make_async_copy(b_in, bulk, load_sem.at[5]),
    ]
    for load in loads:
        load.start()

    barrier = pltpu.get_barrier_semaphore()
    for f in faces:

        @pl.when(has[f])
        def _(f=f):
            pl.semaphore_signal(barrier, inc=1, device_id=other[f], device_id_type=MESH_ID)

    is_sender = (me[2] == root) | (me[2] == root - 1)
    my_sender = jnp.where(me[2] >= root, root, root - 1)

    def greet(t, _):
        @pl.when((t != tile) | (me[2] != my_sender))
        def _():
            pl.semaphore_signal(
                barrier, inc=1, device_id=(t // n_y, t % n_y, my_sender), device_id_type=MESH_ID
            )

        return 0

    lax.fori_loop(0, tiles, greet, 0)

    for side in (0, 1):

        @pl.when(jnp.logical_not(has[0, side]))
        def _(side=side):
            at = 0 if side == 0 else rows_x + 2
            p_ext[:, pl.ds(at, 2), :, :] = jnp.zeros_like(p_ext[:, pl.ds(at, 2), :, :])
            one = 0 if side == 0 else rows_x + 1
            vx[one] = jnp.zeros_like(vx[one])
            inv[one] = jnp.zeros_like(inv[one])

        @pl.when(jnp.logical_not(has[1, side]))
        def _(side=side):
            y_recv[:, side] = jnp.zeros_like(y_recv[:, side])
            yi_recv[side] = jnp.zeros_like(yi_recv[side])

        @pl.when(jnp.logical_not(has[2, side]))
        def _(side=side):
            z_recv[:, side] = jnp.zeros_like(z_recv[:, side])
            zi_recv[side] = jnp.zeros_like(zi_recv[side])

    lane = lax.broadcasted_iota(jnp.int32, (8, depth), 1)
    quad = lane & 3
    group = lane >> 2

    def packed(read):
        q = jnp.zeros((8, depth), F32)
        for j in range(rows_x * halves):
            rolled = pltpu.roll(read(j // halves, (j % halves) * 8), (4 * j + 2) % depth, 1)
            q = jnp.where(group == j, rolled, q)
        return q

    def unpack(tile_value, ref):
        for j in range(rows_x * halves):
            ref[j // halves, pl.ds((j % halves) * 8, 8), :] = pltpu.roll(
                tile_value, (-(4 * j + 2)) % depth, 1
            )

    def coefs(level):
        first = root * depth
        last_ocean = level == first - 1
        crust = level == first
        up = jnp.where(crust, 1.0, 0.5).astype(F32)
        mid = jnp.where(last_ocean, 0.5, jnp.where(crust, -1.5, 0.0)).astype(F32)
        low = jnp.where(last_ocean, -1.0, jnp.where(crust, 0.5, -0.5)).astype(F32)
        return up, mid, low

    row_lane = lax.broadcasted_iota(jnp.int32, (1, 1, depth), 2)
    up, mid, low = coefs(me[2] * depth + row_lane)
    up_e, mid_e, low_e = coefs(
        jnp.where(quad == 1, me[2] * depth - 1, (me[2] + 1) * depth)
    )

    def copy_x(s, side, to):
        src, dst = (2, rows_x + 2) if side == 0 else (rows_x, 0)
        return pltpu.make_async_remote_copy(
            src_ref=p_ext.at[s, pl.ds(src, 2), y_in],
            dst_ref=p_ext.at[s, pl.ds(dst, 2), y_in],
            send_sem=send_sem.at[s, side],
            recv_sem=recv_sem.at[s, 1 - side],
            device_id=to,
            device_id_type=MESH_ID,
        )

    def copy_y(s, side, to):
        return pltpu.make_async_remote_copy(
            src_ref=y_send.at[s, side],
            dst_ref=y_recv.at[s, 1 - side],
            send_sem=send_sem.at[s, 2 + side],
            recv_sem=recv_sem.at[s, 3 - side],
            device_id=to,
            device_id_type=MESH_ID,
        )

    def copy_z(s, side, to):
        return pltpu.make_async_remote_copy(
            src_ref=z_send.at[s],
            dst_ref=z_recv.at[s, 1 - side],
            send_sem=send_sem.at[s, 4 + side],
            recv_sem=recv_sem.at[s, 5 - side],
            device_id=to,
            device_id_type=MESH_ID,
        )

    step_copies = {0: copy_x, 1: copy_y, 2: copy_z}

    def init_copy(src, dst, to, n, back):
        return pltpu.make_async_remote_copy(
            src_ref=src,
            dst_ref=dst,
            send_sem=init_send.at[n],
            recv_sem=init_recv.at[back],
            device_id=to,
            device_id_type=MESH_ID,
        )

    def init_copies(a, side, to):
        if a == 0:
            src, dst = (0, rows_x + 1) if side == 0 else (rows_x - 1, 0)
            return [
                init_copy(
                    v_in.at[0, pl.ds(src, 1)], vx.at[pl.ds(dst, 1)], to, side, 1 - side
                ),
                init_copy(
                    inv.at[pl.ds(src + 1, 1)], inv.at[pl.ds(dst, 1)], to, 6 + side, 7 - side
                ),
            ]
        if a == 1:
            return [init_copy(yi_send.at[side], yi_recv.at[1 - side], to, 2 + side, 3 - side)]
        return [init_copy(zi_send, zi_recv.at[1 - side], to, 4 + side, 5 - side)]

    def send(s):
        z_send[s] = packed(lambda x, y: p_ext[s, 2 + x, pl.ds(YA + y, 8), :])
        y_send[s, 0] = p_ext[s, 2 : rows_x + 2, YA : YA + 2, :]
        y_send[s, 1] = p_ext[s, 2 : rows_x + 2, YA + rows_y - 2 : YA + rows_y, :]
        for f in faces:

            @pl.when(has[f])
            def _(f=f):
                step_copies[f[0]](s, f[1], other[f]).start()

    def receive(s):
        for f in faces:

            @pl.when(has[f])
            def _(f=f):
                step_copies[f[0]](s, 1 - f[1], other[f]).wait_recv()

        p_ext[s, 2 : rows_x + 2, YA - 2 : YA, :] = y_recv[s, 0]
        p_ext[s, 2 : rows_x + 2, YA + rows_y : YA + rows_y + 2, :] = y_recv[s, 1]

    def update(s, sea, end):
        own = z_send[s]
        halo = jnp.where(quad < 2, z_recv[s, 0], z_recv[s, 1])
        sea = sea + jnp.where(
            me[2] >= root,
            jnp.where(quad == 2, own, halo),
            jnp.where(quad == 2, halo, own),
        )
        above = pltpu.roll(jnp.where(quad == 2, own, halo), depth - 1, 1)
        below = pltpu.roll(jnp.where(quad == 1, own, halo), 1, 1)
        edge = vz_edge[...] - 0.5 * pack_edge[...] * (
            up_e * above + mid_e * halo + low_e * below
        )
        vz_edge[...] = edge
        unpack(halo, fill_p)
        unpack(edge, fill_v)

        if end is not None:
            end(sea)

        def along_x(i, _):
            at = pl.ds(i * 3, 3)
            ahead = p_ext[s, pl.ds(i * 3 + 2, 3), y_in, :]
            behind = p_ext[s, pl.ds(i * 3, 3), y_in, :]
            vx[at] = vx[at] - 0.25 * inv[at] * (ahead - behind)
            return 0

        for i in range((rows_x + 2) // 3):
            along_x(i, 0)
        inner = slice(2, rows_x + 2)
        vy[:, YA - 1 : YA, :] = vy[:, YA - 1 : YA, :] - 0.25 * inv_y[0] * (
            p_ext[s, inner, YA : YA + 1, :] - p_ext[s, inner, YA - 2 : YA - 1, :]
        )
        end_y = YA + rows_y
        vy[:, end_y : end_y + 1, :] = vy[:, end_y : end_y + 1, :] - 0.25 * inv_y[1] * (
            p_ext[s, inner, end_y + 1 : end_y + 2, :] - p_ext[s, inner, end_y - 1 : end_y, :]
        )
        chunk = 4
        for i in range(0, rows_x, chunk):
            at = pl.ds(i, chunk)
            at_p = pl.ds(i + 2, chunk)
            here = p_ext[s, at_p, y_in, :]
            rho = inv[pl.ds(i + 1, chunk)]
            vy[at, y_in, :] = vy[at, y_in, :] - 0.25 * rho * (
                p_ext[s, at_p, pl.ds(YA + 1, rows_y), :] - p_ext[s, at_p, pl.ds(YA - 1, rows_y), :]
            )
            halo_p = fill_p[at]
            above_p = pltpu.roll(jnp.where(row_lane == 0, halo_p, here), depth - 1, 2)
            below_p = pltpu.roll(jnp.where(row_lane == depth - 1, halo_p, here), 1, 2)
            vz[at] = vz[at] - 0.5 * rho * (up * above_p + mid * here + low * below_p)
        for i in range(0, rows_x, chunk):
            at = pl.ds(i, chunk)
            at_p = pl.ds(i + 2, chunk)
            w = vz[at]
            halo_v = fill_v[at]
            above_v = pltpu.roll(jnp.where(row_lane == 0, halo_v, w), depth - 1, 2)
            below_v = pltpu.roll(jnp.where(row_lane == depth - 1, halo_v, w), 1, 2)
            spread = (
                0.5 * (vx[pl.ds(i + 2, chunk)] - vx[at])
                + 0.5 * (vy[at, pl.ds(YA + 1, rows_y), :] - vy[at, pl.ds(YA - 1, rows_y), :])
                + (up * above_v + mid * w + low * below_v)
            )
            added = jnp.where(row_lane == 0, pltpu.roll(source[at], (depth - s) % depth, 2), 0.0)
            p_ext[s + 1, at_p, y_in, :] = p_ext[s, at_p, y_in, :] - 0.5 * bulk[at] * spread + added
        return sea

    for load in loads:
        load.wait()
    zi_send[0] = packed(lambda x, y: vz[x, pl.ds(y, 8), :])
    zi_send[1] = packed(lambda x, y: inv[1 + x, pl.ds(y, 8), :])
    for side, y in ((0, 0), (1, rows_y - 1)):
        yi_send[side, :, 0:1, :] = vy[:, YA + y : YA + y + 1, :]
        yi_send[side, :, 1:2, :] = inv[1 : rows_x + 1, y : y + 1, :]
    count = sum(has[f].astype(jnp.int32) for f in faces)
    owners_z = jnp.where(me[2] == root, n_z - root, jnp.where(me[2] == root - 1, root, 0))
    count = count + jnp.where(is_sender, owners_z * tiles - 1, 0)
    pl.semaphore_wait(barrier, count)
    send(0)
    for f in faces:

        @pl.when(has[f])
        def _(f=f):
            for copy in init_copies(*f, other[f]):
                copy.start()

    cell_x = gx_ref[...] - me[0] * rows_x
    cell_y = gy_ref[...] - me[1] * rows_y
    inside = (cell_x >= 0) & (cell_x < rows_x) & (cell_y >= 0) & (cell_y < rows_y)
    cell = jnp.where(inside, cell_x * rows_y + cell_y, -1)
    gauges = cell.shape[1]
    hot = (lax.broadcasted_iota(jnp.int32, (cells, gauges), 0) == cell).astype(F32)
    scaled = misfit_ref[...] * jnp.where(me[2] == 0, 0.5, 0.0).astype(F32)
    scaled = jnp.concatenate([scaled, jnp.zeros((depth - ITERS, gauges), F32)], axis=0)
    planes = lax.dot_general(hot, scaled, NT, precision=HIGHEST, preferred_element_type=F32)
    source[...] = planes.reshape(rows_x, rows_y, depth)

    nodes = patch_ref.shape[-1]
    patches = slot_ref.shape[1]
    per = patches // tiles
    shift = per.bit_length() - 1
    assert per == 1 << shift and per == 128
    block = min(patches, 1024)
    patch = patch_ref[...].reshape(1, nodes)
    slot_parts = jnp.zeros((8, nodes), F32)
    first_row = lax.broadcasted_iota(jnp.int32, (8, block), 0) == 0
    for at in range(0, patches, block):
        slots = slot_ref[:, at : at + block]
        table = jnp.where(first_row, slots >> shift, slots & (per - 1)).astype(F32)
        hot = lax.broadcasted_iota(jnp.int32, (block, nodes), 0) + at == patch
        slot_parts = slot_parts + jnp.dot(
            table.astype(jnp.bfloat16),
            hot.astype(F32).astype(jnp.bfloat16),
            preferred_element_type=F32,
        )
    slot = (slot_parts[0:1] * per + slot_parts[1:2]).astype(jnp.int32)
    for at in range(0, patches, block):
        hot = lax.broadcasted_iota(jnp.int32, (block, nodes), 0) + at == slot
        slot_hot[pl.ds(at, block), :] = hot.astype(F32).astype(jnp.bfloat16)
    node = lax.broadcasted_iota(jnp.int32, (depth, nodes), 1)
    spread_hot[...] = (
        lax.broadcasted_iota(jnp.int32, (depth, nodes), 0) == 4 * (node >> 3) + 2
    ).astype(F32)

    def slip_copy(o, c):
        return pltpu.make_async_remote_copy(
            src_ref=part.at[o],
            dst_ref=got.at[tile],
            send_sem=slip_send.at[o, c],
            recv_sem=slip_recv.at[tile],
            device_id=(o // n_y, o % n_y, c),
            device_id_type=MESH_ID,
        )

    def to_owners(act):
        def one(n, _):
            o = n // n_z
            c = n % n_z
            mine = (c >= root) == (me[2] >= root)

            @pl.when(mine & ((o != tile) | (c != me[2])))
            def _():
                act(slip_copy(o, c))

            return 0

        lax.fori_loop(0, tiles * n_z, one, 0)

    def finish_sea(sea):
        @pl.when(is_sender)
        def _():
            total = 0.5 * (sea + pltpu.roll(sea, 1, 1))
            values = jnp.dot(total, spread_hot[...], precision=HIGHEST, preferred_element_type=F32)
            sub = lax.broadcasted_iota(jnp.int32, (8, nodes), 0)
            col = lax.broadcasted_iota(jnp.int32, (8, nodes), 1)
            row = jnp.sum(jnp.where((col & 7) == sub, values, 0.0), axis=0, keepdims=True)
            row = row * weight_ref[...].reshape(1, nodes)
            high = row.astype(jnp.bfloat16).astype(F32)
            rest = row - high
            middle = rest.astype(jnp.bfloat16).astype(F32)
            lowest = rest - middle
            split = jnp.where(
                sub == 0, high, jnp.where(sub == 1, middle, jnp.where(sub == 2, lowest, 0.0))
            ).astype(jnp.bfloat16)
            for at in range(0, patches, block):
                sums = lax.dot_general(
                    split, slot_hot[pl.ds(at, block), :], NT, preferred_element_type=F32
                )
                sums = jnp.sum(sums, axis=0, keepdims=True)
                for o in range(block // per):
                    part[at // per + o] = sums[:, o * per : (o + 1) * per]
            got[tile] = part[tile]
            to_owners(lambda copy: copy.start())

    for f in faces:

        @pl.when(has[f])
        def _(f=f):
            for copy in init_copies(f[0], 1 - f[1], other[f]):
                copy.wait_recv()

    for side, y in ((0, YA - 1), (1, YA + rows_y)):
        vy[:, y : y + 1, :] = yi_recv[side, :, 0:1, :]
        inv_y[side] = yi_recv[side, :, 1:2, :]
    kept = (quad == 1) | (quad == 2)
    vz_edge[...] = jnp.where(
        kept, jnp.where(quad == 1, zi_recv[0, 0], zi_recv[1, 0]), 0.0
    )
    pack_edge[...] = jnp.where(
        kept, jnp.where(quad == 1, zi_recv[0, 1], zi_recv[1, 1]), 0.0
    )

    receive(0)
    sea = update(0, jnp.zeros((8, depth), F32), None)
    for s in range(1, ITERS):
        send(s)
        receive(s)
        sea = update(s, sea, finish_sea if s == ITERS - 1 else None)

    stores = [
        pltpu.make_async_copy(vx.at[pl.ds(1, rows_x)], v_out.at[0], store_sem.at[0]),
        pltpu.make_async_copy(vy.at[:, y_in], v_out.at[1], store_sem.at[1]),
        pltpu.make_async_copy(vz, v_out.at[2], store_sem.at[2]),
        pltpu.make_async_copy(p_ext.at[ITERS, x_in, y_in], p_out, store_sem.at[3]),
    ]
    for store in stores:
        store.start()

    def arrive(t, _):
        @pl.when((t != tile) | (me[2] != my_sender))
        def _():
            pltpu.make_async_remote_copy(
                src_ref=part.at[0],
                dst_ref=got.at[t],
                send_sem=slip_send.at[0, 0],
                recv_sem=slip_recv.at[t],
                device_id=(t // n_y, t % n_y, my_sender),
                device_id_type=MESH_ID,
            ).wait_recv()

        return 0

    lax.fori_loop(0, tiles, arrive, 0)
    total = jnp.sum(got[...], axis=0)
    piece = per // n_z
    picked = total[:, 0:piece]
    for c in range(1, n_z):
        picked = jnp.where(me[2] == c, total[:, c * piece : (c + 1) * piece], picked)
    slip_out[...] = picked

    for f in faces:

        @pl.when(has[f])
        def _(f=f):
            for copy in init_copies(*f, other[f]):
                copy.wait_send()
            for s in range(ITERS):
                step_copies[f[0]](s, f[1], other[f]).wait_send()

    @pl.when(is_sender)
    def _():
        to_owners(lambda copy: copy.wait_send())

    for store in stores:
        store.wait()


def local(sizes, pressure, velocity, inv_density, bulk, node_weight, node_patch, patch_slot,
          gauge_x, gauge_y, gauge_misfit):
    rows_x, rows_y, depth = pressure.shape
    n_x, n_y, n_z = sizes
    tiles = n_x * n_y
    nodes = node_patch.shape[-1]
    patches = patch_slot.shape[0]
    per = patches // tiles
    wide_y = rows_y + 2 * YA
    box = (rows_x, rows_y, depth)
    vmem = pl.BlockSpec(memory_space=pltpu.VMEM)
    hbm = pl.BlockSpec(memory_space=pl.ANY)
    scratch = [
        pltpu.VMEM((ITERS + 1, rows_x + 4, wide_y, depth), F32),
        pltpu.VMEM((rows_x + 2, rows_y, depth), F32),
        pltpu.VMEM((rows_x, wide_y, depth), F32),
        pltpu.VMEM(box, F32),
        pltpu.VMEM((rows_x + 2, rows_y, depth), F32),
        pltpu.VMEM((2, rows_x, 1, depth), F32),
        pltpu.VMEM(box, F32),
        pltpu.VMEM((8, depth), F32),
        pltpu.VMEM((8, depth), F32),
        pltpu.VMEM(box, F32),
        pltpu.VMEM(box, F32),
        pltpu.VMEM((ITERS, 2, rows_x, 2, depth), F32),
        pltpu.VMEM((ITERS, 2, rows_x, 2, depth), F32),
        pltpu.VMEM((ITERS, 8, depth), F32),
        pltpu.VMEM((ITERS, 2, 8, depth), F32),
        pltpu.VMEM((2, rows_x, 2, depth), F32),
        pltpu.VMEM((2, rows_x, 2, depth), F32),
        pltpu.VMEM((2, 8, depth), F32),
        pltpu.VMEM((2, 2, 8, depth), F32),
        pltpu.VMEM(box, F32),
        pltpu.VMEM((patches, nodes), jnp.bfloat16),
        pltpu.VMEM((depth, nodes), F32),
        pltpu.VMEM((tiles, 1, per), F32),
        pltpu.VMEM((tiles, 1, per), F32),
        pltpu.SemaphoreType.DMA((6,)),
        pltpu.SemaphoreType.DMA((4,)),
        pltpu.SemaphoreType.DMA((ITERS, 6)),
        pltpu.SemaphoreType.DMA((ITERS, 6)),
        pltpu.SemaphoreType.DMA((8,)),
        pltpu.SemaphoreType.DMA((8,)),
        pltpu.SemaphoreType.DMA((tiles, n_z)),
        pltpu.SemaphoreType.DMA((tiles,)),
    ]
    p_new, v_new, slip = pl.pallas_call(
        functools.partial(kernel, sizes),
        out_shape=[
            jax.ShapeDtypeStruct(box, F32),
            jax.ShapeDtypeStruct((3,) + box, F32),
            jax.ShapeDtypeStruct((1, per // n_z), F32),
        ],
        in_specs=[hbm] * 4 + [vmem] * 6,
        out_specs=[hbm, hbm, vmem],
        scratch_shapes=scratch,
        compiler_params=pltpu.CompilerParams(
            collective_id=0, has_side_effects=True, vmem_limit_bytes=32 * 1024 * 1024
        ),
    )(
        pressure,
        velocity,
        inv_density,
        bulk,
        node_weight,
        node_patch,
        patch_slot.reshape(1, patches),
        gauge_x.reshape(1, -1),
        gauge_y.reshape(1, -1),
        gauge_misfit,
    )
    return p_new, v_new, slip.reshape(per // n_z)


def solution(mesh):
    placed = (
        P("gx", "gy", "gz"),
        P(None, "gx", "gy", "gz"),
        P("gx", "gy", "gz"),
        P("gx", "gy", "gz"),
        P("gx", "gy", None),
        P("gx", "gy", None),
        P(),
        P(),
        P(),
        P(),
    )
    sizes = tuple(mesh.shape[a] for a in AXES)
    return jax.shard_map(
        functools.partial(local, sizes),
        mesh=mesh,
        in_specs=placed,
        out_specs=(P("gx", "gy", "gz"), P(None, "gx", "gy", "gz"), P(("gx", "gy", "gz"))),
        check_vma=False,
    )
```

time: 218 us -> 34.4 us (0.16)
  local copies, waits for them, and re-layouts: 84.7 us -> 9.02 us
  starting transfers between devices: 59 us -> 0 us
  other arithmetic: 51.4 us -> 0 us
  Pallas kernels: 0 us -> 24.4 us
  blocking collectives: 12.9 us -> 0 us
  waiting for transfers between devices: 6.94 us -> 0 us
    ppermute x18 -> x0, starting transfers between devices: 47.7 us -> none  [the longest x9 36 us: extended(): lax.ppermute(lax.slice_in_dim(block, block.shape[dim] - width, None, axis...]
    ppermute x12 -> x0, local copies, waits for them, and re-layouts: 33.5 us -> none  [the longest x6 17.3 us: extended(): lax.ppermute(lax.slice_in_dim(block, 0, width, axis=dim), axis, backward)]
    concatenate x10 -> x0, other arithmetic: 28.4 us -> none  [the longest x9 27.5 us: extended(): block = jnp.concatenate([low, block, high], axis=dim)]
    pallas_call x0 -> x1, Pallas kernels: none -> 24.4 us  [local(): pl.pallas_call(functools.partial(kernel, sizes), out_shape=[jax.ShapeDtyp...]
    concatenate x6 -> x0, local copies, waits for them, and re-layouts: 21.8 us -> none  [extended(): block = jnp.concatenate([low, block, high], axis=dim)]
    psum x1 -> x0, blocking collectives: 12.9 us -> none  [spread_2(): return lax.psum(kept, axis)]
    all_to_all x2 -> x0, starting transfers between devices: 11.3 us -> none  [the longest x1 7.07 us: local(): lax.all_to_all(send_ids, ('gx', 'gy'), split_axis=0, concat_axis=0, tiled...]
    gather x5 -> x0, local copies, waits for them, and re-layouts: 9.4 us -> none  [the longest x1 2.61 us: local(): sorted_owner = owners[order]]
  transfers between devices with their start and end apart: 20 -> 0, of which waited for: 3 -> 0; matrix products, arithmetic and copies ran while one was open for 44% -> 0% of each run, Pallas kernels for 0% -> 0%
where the time goes in v1:
time: 34.4 us; the launch traced here: 34.1 us
  Pallas kernels  24.4 us (71%)
  local copies, waits for them, and re-layouts  9.02 us (26%)
  between operations  0.67 us (2%)
    pallas_call x1, Pallas kernels, local(): pl.pallas_call(functools.partial(kernel, sizes), out_shape=[jax.ShapeDtyp...  24.4 us
    unnamed x23, local copies, waits for them, and re-layouts  9.02 us

profile of v1, /device:TPU:0, one launch (start us, length us, event | category | flops | bytes accessed | tf_op | source)
XLA Modules:
  0.0 34.1 jit_solution(7773190445391212652)
XLA Ops:
  0.6 0.0 copy-start.4
  0.6 0.0 copy-start.6
  0.7 0.7 %copy-done.4 = s32[1024]{0:T(1024)S(1)} copy-done((s32[1024]{0:T(1024)S(1)}, s32[1024]{0:T(1024)}, u32[]{:S(2)}) %copy-start.4) | copy-done | bytes 4120
  1.3 0.0 copy-done.6
  1.3 0.0 copy-start
  1.3 1.0 %copy-done = f32[3,16,16,128]{3,2,1,0:T(8,128)S(1)} copy-done((f32[3,16,16,128]{3,2,1,0:T(8,128)S(1)}, f32[3,16,16,128]{3,2,1,0:T(8,128)}, u32[]{:S(2)}) %copy-start) | copy-done | bytes 393240
  2.3 0.0 copy-start.1
  2.3 0.9 %copy-done.1 = f32[16,16,128]{2,1,0:T(8,128)S(1)} copy-done((f32[16,16,128]{2,1,0:T(8,128)S(1)}, f32[16,16,128]{2,1,0:T(8,128)}, u32[]{:S(2)}) %copy-start.1) | copy-done | bytes 131096
  3.2 0.0 copy-start.2
  3.2 0.9 %copy-done.2 = f32[16,16,128]{2,1,0:T(8,128)S(1)} copy-done((f32[16,16,128]{2,1,0:T(8,128)S(1)}, f32[16,16,128]{2,1,0:T(8,128)}, u32[]{:S(2)}) %copy-start.2) | copy-done | bytes 131096
  4.1 0.0 copy-start.3
  4.1 0.9 %copy-done.3 = f32[16,16,128]{2,1,0:T(8,128)S(1)} copy-done((f32[16,16,128]{2,1,0:T(8,128)S(1)}, f32[16,16,128]{2,1,0:T(8,128)}, u32[]{:S(2)}) %copy-start.3) | copy-done | bytes 131096
  5.0 0.0 copy-start.5
  5.0 0.7 %copy-done.5 = f32[4,256]{1,0:T(4,128)S(1)} copy-done((f32[4,256]{1,0:T(4,128)S(1)}, f32[4,256]{1,0:T(4,128)}, u32[]{:S(2)}) %copy-start.5) | copy-done | bytes 4120
  5.7 0.0 copy-start.7
  5.7 0.7 %copy-done.7 = s32[1,1,256]{2,1,0:T(1,128)S(1)} copy-done((s32[1,1,256]{2,1,0:T(1,128)S(1)}, s32[1,1,256]{2,1,0:T(1,128)}, u32[]{:S(2)}) %copy-start.7) | copy-done | bytes 1048
  6.4 0.0 copy-start.8
  6.4 0.7 %copy-done.8 = s32[256]{0:T(256)S(1)} copy-done((s32[256]{0:T(256)S(1)}, s32[256]{0:T(256)}, u32[]{:S(2)}) %copy-start.8) | copy-done | bytes 1048
  7.1 0.0 copy-start.9
  7.1 0.7 %copy-done.9 = s32[256]{0:T(256)S(1)} copy-done((s32[256]{0:T(256)S(1)}, s32[256]{0:T(256)}, u32[]{:S(2)}) %copy-start.9) | copy-done | bytes 1048
  7.8 24.4 %shard_map.121 = (f32[16,16,128]{2,1,0:T(8,128)S(1)}, f32[3,16,16,128]{3,2,1,0:T(8,128)S(1)}, f32[1,32]{1,0:T(1,128)S(1)}) custom-call(f32[16,16,128]{2,1,0:T(8,128)S(1)} %copy-done.1, f32[3,16,16,128]{3,2,1,0:T(8,128)S(1)} %copy-done, f32[16,16,128]{2,1,0:T(8,128)S(1)} %copy-done.2, f32[16,16,128]{2,1,0:T(8,128)S(1)} %copy-done.3, ...), custom_call_target="tpu_custom_call" | custom-call | tf_op jit(solution)/shard_map/pallas_call | solution.py:542
  32.2 0.7 %copy.16 = f32[16,16,128]{2,1,0:T(8,128)} copy(f32[16,16,128]{2,1,0:T(8,128)S(1)} %get-tuple-element.12) | data formatting | bytes 262144
  32.9 0.7 %copy.17 = f32[3,16,16,128]{3,2,1,0:T(8,128)} copy(f32[3,16,16,128]{3,2,1,0:T(8,128)S(1)} %get-tuple-element.13) | data formatting | bytes 786432
  33.6 0.5 %copy.18 = f32[32]{0:T(128)} copy(f32[32]{0:T(128)S(1)} %bitcast.7) | data formatting | bytes 256
Async XLA Ops:
  0.6 0.7 %copy-start.4 = (s32[1024]{0:T(1024)S(1)}, s32[1024]{0:T(1024)}, u32[]{:S(2)}) copy-start(s32[1024]{0:T(1024)} %param.16) | copy-start | bytes 12292
  0.6 0.7 %copy-start.6 = (f32[1,1,256]{2,1,0:T(1,128)S(1)}, f32[1,1,256]{2,1,0:T(1,128)}, u32[]{:S(2)}) copy-start(f32[1,1,256]{2,1,0:T(1,128)} %weight_ref.1) | copy-start | bytes 3076
  1.3 1.0 %copy-start = (f32[3,16,16,128]{3,2,1,0:T(8,128)S(1)}, f32[3,16,16,128]{3,2,1,0:T(8,128)}, u32[]{:S(2)}) copy-start(f32[3,16,16,128]{3,2,1,0:T(8,128)} %v_in.1) | copy-start | bytes 1179652
  2.3 0.9 %copy-start.1 = (f32[16,16,128]{2,1,0:T(8,128)S(1)}, f32[16,16,128]{2,1,0:T(8,128)}, u32[]{:S(2)}) copy-start(f32[16,16,128]{2,1,0:T(8,128)} %p_in.1) | copy-start | bytes 393220
  3.2 0.9 %copy-start.2 = (f32[16,16,128]{2,1,0:T(8,128)S(1)}, f32[16,16,128]{2,1,0:T(8,128)}, u32[]{:S(2)}) copy-start(f32[16,16,128]{2,1,0:T(8,128)} %d_in.1) | copy-start | bytes 393220
  4.1 0.9 %copy-start.3 = (f32[16,16,128]{2,1,0:T(8,128)S(1)}, f32[16,16,128]{2,1,0:T(8,128)}, u32[]{:S(2)}) copy-start(f32[16,16,128]{2,1,0:T(8,128)} %b_in.1) | copy-start | bytes 393220
  5.0 0.7 %copy-start.5 = (f32[4,256]{1,0:T(4,128)S(1)}, f32[4,256]{1,0:T(4,128)}, u32[]{:S(2)}) copy-start(f32[4,256]{1,0:T(4,128)} %misfit_ref.1) | copy-start | bytes 12292
  5.7 0.7 %copy-start.7 = (s32[1,1,256]{2,1,0:T(1,128)S(1)}, s32[1,1,256]{2,1,0:T(1,128)}, u32[]{:S(2)}) copy-start(s32[1,1,256]{2,1,0:T(1,128)} %patch_ref.1) | copy-start | bytes 3076
  6.4 0.7 %copy-start.8 = (s32[256]{0:T(256)S(1)}, s32[256]{0:T(256)}, u32[]{:S(2)}) copy-start(s32[256]{0:T(256)} %param.17) | copy-start | bytes 3076
  7.1 0.7 %copy-start.9 = (s32[256]{0:T(256)S(1)}, s32[256]{0:T(256)}, u32[]{:S(2)}) copy-start(s32[256]{0:T(256)} %param.18) | copy-start | bytes 3076

commit v2 on v1

--- a/solution.py
+++ b/solution.py
@@ -22,15 +22,21 @@
     v_in,
     d_in,
     b_in,
+    weight_in,
+    patch_in,
+    slot_in,
+    gx_in,
+    gy_in,
+    misfit_in,
+    p_out,
+    v_out,
+    slip_out,
     weight_ref,
     patch_ref,
     slot_ref,
     gx_ref,
     gy_ref,
     misfit_ref,
-    p_out,
-    v_out,
-    slip_out,
     p_ext,
     vx,
     vy,
@@ -55,14 +61,17 @@
     spread_hot,
     part,
     got,
+    total,
+    got_all,
     load_sem,
-    store_sem,
     send_sem,
     recv_sem,
     init_send,
     init_recv,
     slip_send,
     slip_recv,
+    depth_send,
+    depth_recv,
 ):
     n_x, n_y, n_z = sizes
     rows_x, rows_y, depth = p_in.shape
@@ -92,6 +101,12 @@
         pltpu.make_async_copy(v_in.at[1], vy.at[:, y_in], load_sem.at[3]),
         pltpu.make_async_copy(v_in.at[0], vx.at[pl.ds(1, rows_x)], load_sem.at[4]),
         pltpu.make_async_copy(b_in, bulk, load_sem.at[5]),
+        pltpu.make_async_copy(weight_in, weight_ref, load_sem.at[6]),
+        pltpu.make_async_copy(patch_in, patch_ref, load_sem.at[7]),
+        pltpu.make_async_copy(slot_in, slot_ref, load_sem.at[8]),
+        pltpu.make_async_copy(gx_in, gx_ref, load_sem.at[9]),
+        pltpu.make_async_copy(gy_in, gy_ref, load_sem.at[10]),
+        pltpu.make_async_copy(misfit_in, misfit_ref, load_sem.at[11]),
     ]
     for load in loads:
         load.start()
@@ -103,19 +118,44 @@
         def _(f=f):
             pl.semaphore_signal(barrier, inc=1, device_id=other[f], device_id_type=MESH_ID)
 
-    is_sender = (me[2] == root) | (me[2] == root - 1)
-    my_sender = jnp.where(me[2] >= root, root, root - 1)
-
-    def greet(t, _):
-        @pl.when((t != tile) | (me[2] != my_sender))
-        def _():
+    at_sea = (me[2] == root) | (me[2] == root - 1)
+
+    def each_tile(act):
+        def one(o_x, o_y):
+            @pl.when((o_x != me[0]) | (o_y != me[1]))
+            def _():
+                act(o_x, o_y)
+
+        if tiles <= 8:
+            for o in range(tiles):
+                one(o // n_y, o % n_y)
+        else:
+
+            def row(o_x, _):
+                def column(o_y, _):
+                    one(o_x, o_y)
+                    return 0
+
+                return lax.fori_loop(0, n_y, column, 0)
+
+            lax.fori_loop(0, n_x, row, 0)
+
+    def greet(o_x, o_y):
+        pl.semaphore_signal(
+            barrier, inc=1, device_id=(o_x, o_y, me[2]), device_id_type=MESH_ID
+        )
+
+    @pl.when(at_sea)
+    def _():
+        each_tile(greet)
+
+    for c in (root - 1, root):
+
+        @pl.when(me[2] != c)
+        def _(c=c):
             pl.semaphore_signal(
-                barrier, inc=1, device_id=(t // n_y, t % n_y, my_sender), device_id_type=MESH_ID
+                barrier, inc=1, device_id=(me[0], me[1], c), device_id_type=MESH_ID
             )
-
-        return 0
-
-    lax.fori_loop(0, tiles, greet, 0)
 
     for side in (0, 1):
 
@@ -247,14 +287,9 @@
         p_ext[s, 2 : rows_x + 2, YA - 2 : YA, :] = y_recv[s, 0]
         p_ext[s, 2 : rows_x + 2, YA + rows_y : YA + rows_y + 2, :] = y_recv[s, 1]
 
-    def update(s, sea, end):
+    def update(s, last):
         own = z_send[s]
         halo = jnp.where(quad < 2, z_recv[s, 0], z_recv[s, 1])
-        sea = sea + jnp.where(
-            me[2] >= root,
-            jnp.where(quad == 2, own, halo),
-            jnp.where(quad == 2, halo, own),
-        )
         above = pltpu.roll(jnp.where(quad == 2, own, halo), depth - 1, 1)
         below = pltpu.roll(jnp.where(quad == 1, own, halo), 1, 1)
         edge = vz_edge[...] - 0.5 * pack_edge[...] * (
@@ -263,9 +298,6 @@
         vz_edge[...] = edge
         unpack(halo, fill_p)
         unpack(edge, fill_v)
-
-        if end is not None:
-            end(sea)
 
         def along_x(i, _):
             at = pl.ds(i * 3, 3)
@@ -297,6 +329,11 @@
             above_p = pltpu.roll(jnp.where(row_lane == 0, halo_p, here), depth - 1, 2)
             below_p = pltpu.roll(jnp.where(row_lane == depth - 1, halo_p, here), 1, 2)
             vz[at] = vz[at] - 0.5 * rho * (up * above_p + mid * here + low * below_p)
+        if last:
+            v_out[0] = vx[1 : rows_x + 1]
+            v_out[1] = vy[:, YA : YA + rows_y, :]
+            v_out[2] = vz[...]
+            owner_sums()
         for i in range(0, rows_x, chunk):
             at = pl.ds(i, chunk)
             at_p = pl.ds(i + 2, chunk)
@@ -310,8 +347,11 @@
                 + (up * above_v + mid * w + low * below_v)
             )
             added = jnp.where(row_lane == 0, pltpu.roll(source[at], (depth - s) % depth, 2), 0.0)
-            p_ext[s + 1, at_p, y_in, :] = p_ext[s, at_p, y_in, :] - 0.5 * bulk[at] * spread + added
-        return sea
+            new = p_ext[s, at_p, y_in, :] - 0.5 * bulk[at] * spread + added
+            if last:
+                p_out[at] = new
+            else:
+                p_ext[s + 1, at_p, y_in, :] = new
 
     for load in loads:
         load.wait()
@@ -321,8 +361,7 @@
         yi_send[side, :, 0:1, :] = vy[:, YA + y : YA + y + 1, :]
         yi_send[side, :, 1:2, :] = inv[1 : rows_x + 1, y : y + 1, :]
     count = sum(has[f].astype(jnp.int32) for f in faces)
-    owners_z = jnp.where(me[2] == root, n_z - root, jnp.where(me[2] == root - 1, root, 0))
-    count = count + jnp.where(is_sender, owners_z * tiles - 1, 0)
+    count = count + jnp.where(at_sea, tiles - 1 + n_z - 1, 0)
     pl.semaphore_wait(barrier, count)
     send(0)
     for f in faces:
@@ -370,35 +409,33 @@
         lax.broadcasted_iota(jnp.int32, (depth, nodes), 0) == 4 * (node >> 3) + 2
     ).astype(F32)
 
-    def slip_copy(o, c):
+    def slip_copy(o_x, o_y, source_tile):
         return pltpu.make_async_remote_copy(
-            src_ref=part.at[o],
-            dst_ref=got.at[tile],
-            send_sem=slip_send.at[o, c],
-            recv_sem=slip_recv.at[tile],
-            device_id=(o // n_y, o % n_y, c),
+            src_ref=part.at[o_x * n_y + o_y],
+            dst_ref=got.at[source_tile],
+            send_sem=slip_send.at[o_x * n_y + o_y],
+            recv_sem=slip_recv.at[source_tile],
+            device_id=(o_x, o_y, me[2]),
             device_id_type=MESH_ID,
         )
 
-    def to_owners(act):
-        def one(n, _):
-            o = n // n_z
-            c = n % n_z
-            mine = (c >= root) == (me[2] >= root)
-
-            @pl.when(mine & ((o != tile) | (c != me[2])))
-            def _():
-                act(slip_copy(o, c))
-
-            return 0
-
-        lax.fori_loop(0, tiles * n_z, one, 0)
+    def depth_copy(c, slot):
+        return pltpu.make_async_remote_copy(
+            src_ref=total,
+            dst_ref=got_all.at[slot],
+            send_sem=depth_send.at[c],
+            recv_sem=depth_recv.at[slot],
+            device_id=(me[0], me[1], c),
+            device_id_type=MESH_ID,
+        )
+
+    my_slot = jnp.where(me[2] >= root, 1, 0)
 
     def finish_sea(sea):
-        @pl.when(is_sender)
+        @pl.when(at_sea)
         def _():
-            total = 0.5 * (sea + pltpu.roll(sea, 1, 1))
-            values = jnp.dot(total, spread_hot[...], precision=HIGHEST, preferred_element_type=F32)
+            mine = 0.5 * jnp.where(me[2] == root, sea, pltpu.roll(sea, 1, 1))
+            values = jnp.dot(mine, spread_hot[...], precision=HIGHEST, preferred_element_type=F32)
             sub = lax.broadcasted_iota(jnp.int32, (8, nodes), 0)
             col = lax.broadcasted_iota(jnp.int32, (8, nodes), 1)
             row = jnp.sum(jnp.where((col & 7) == sub, values, 0.0), axis=0, keepdims=True)
@@ -418,7 +455,19 @@
                 for o in range(block // per):
                     part[at // per + o] = sums[:, o * per : (o + 1) * per]
             got[tile] = part[tile]
-            to_owners(lambda copy: copy.start())
+            each_tile(lambda o_x, o_y: slip_copy(o_x, o_y, tile).start())
+
+    def owner_sums():
+        @pl.when(at_sea)
+        def _():
+            each_tile(lambda o_x, o_y: slip_copy(o_x, o_y, o_x * n_y + o_y).wait_recv())
+            total[...] = jnp.sum(got[...], axis=0)
+            got_all[my_slot] = total[...]
+            for c in range(n_z):
+
+                @pl.when(me[2] != c)
+                def _(c=c):
+                    depth_copy(c, my_slot).start()
 
     for f in faces:
 
@@ -439,41 +488,27 @@
     )
 
     receive(0)
-    sea = update(0, jnp.zeros((8, depth), F32), None)
+    sea = z_send[0]
+    update(0, False)
     for s in range(1, ITERS):
         send(s)
+        sea = sea + z_send[s]
+        if s == ITERS - 1:
+            finish_sea(sea)
         receive(s)
-        sea = update(s, sea, finish_sea if s == ITERS - 1 else None)
-
-    stores = [
-        pltpu.make_async_copy(vx.at[pl.ds(1, rows_x)], v_out.at[0], store_sem.at[0]),
-        pltpu.make_async_copy(vy.at[:, y_in], v_out.at[1], store_sem.at[1]),
-        pltpu.make_async_copy(vz, v_out.at[2], store_sem.at[2]),
-        pltpu.make_async_copy(p_ext.at[ITERS, x_in, y_in], p_out, store_sem.at[3]),
-    ]
-    for store in stores:
-        store.start()
-
-    def arrive(t, _):
-        @pl.when((t != tile) | (me[2] != my_sender))
-        def _():
-            pltpu.make_async_remote_copy(
-                src_ref=part.at[0],
-                dst_ref=got.at[t],
-                send_sem=slip_send.at[0, 0],
-                recv_sem=slip_recv.at[t],
-                device_id=(t // n_y, t % n_y, my_sender),
-                device_id_type=MESH_ID,
-            ).wait_recv()
-
-        return 0
-
-    lax.fori_loop(0, tiles, arrive, 0)
-    total = jnp.sum(got[...], axis=0)
+        update(s, s == ITERS - 1)
+
+    for slot_at, c in ((0, root - 1), (1, root)):
+
+        @pl.when(me[2] != c)
+        def _(slot_at=slot_at):
+            depth_copy(0, slot_at).wait_recv()
+
+    sums = got_all[0] + got_all[1]
     piece = per // n_z
-    picked = total[:, 0:piece]
+    picked = sums[:, 0:piece]
     for c in range(1, n_z):
-        picked = jnp.where(me[2] == c, total[:, c * piece : (c + 1) * piece], picked)
+        picked = jnp.where(me[2] == c, sums[:, c * piece : (c + 1) * piece], picked)
     slip_out[...] = picked
 
     for f in faces:
@@ -485,12 +520,14 @@
             for s in range(ITERS):
                 step_copies[f[0]](s, f[1], other[f]).wait_send()
 
-    @pl.when(is_sender)
+    @pl.when(at_sea)
     def _():
-        to_owners(lambda copy: copy.wait_send())
-
-    for store in stores:
-        store.wait()
+        each_tile(lambda o_x, o_y: slip_copy(o_x, o_y, tile).wait_send())
+        for c in range(n_z):
+
+            @pl.when(me[2] != c)
+            def _(c=c):
+                depth_copy(c, my_slot).wait_send()
 
 
 def local(sizes, pressure, velocity, inv_density, bulk, node_weight, node_patch, patch_slot,
@@ -504,9 +541,16 @@
     wide_y = rows_y + 2 * YA
     box = (rows_x, rows_y, depth)
     vmem = pl.BlockSpec(memory_space=pltpu.VMEM)
-    hbm = pl.BlockSpec(memory_space=pl.ANY)
+    hbm = pl.BlockSpec(memory_space=pltpu.HBM)
+    gauges = gauge_x.shape[0]
     scratch = [
-        pltpu.VMEM((ITERS + 1, rows_x + 4, wide_y, depth), F32),
+        pltpu.VMEM((1, 1, nodes), F32),
+        pltpu.VMEM((1, 1, nodes), jnp.int32),
+        pltpu.VMEM((1, patches), jnp.int32),
+        pltpu.VMEM((1, gauges), jnp.int32),
+        pltpu.VMEM((1, gauges), jnp.int32),
+        pltpu.VMEM((ITERS, gauges), F32),
+        pltpu.VMEM((ITERS, rows_x + 4, wide_y, depth), F32),
         pltpu.VMEM((rows_x + 2, rows_y, depth), F32),
         pltpu.VMEM((rows_x, wide_y, depth), F32),
         pltpu.VMEM(box, F32),
@@ -530,14 +574,17 @@
         pltpu.VMEM((depth, nodes), F32),
         pltpu.VMEM((tiles, 1, per), F32),
         pltpu.VMEM((tiles, 1, per), F32),
-        pltpu.SemaphoreType.DMA((6,)),
-        pltpu.SemaphoreType.DMA((4,)),
+        pltpu.VMEM((1, per), F32),
+        pltpu.VMEM((2, 1, per), F32),
+        pltpu.SemaphoreType.DMA((12,)),
         pltpu.SemaphoreType.DMA((ITERS, 6)),
         pltpu.SemaphoreType.DMA((ITERS, 6)),
         pltpu.SemaphoreType.DMA((8,)),
         pltpu.SemaphoreType.DMA((8,)),
-        pltpu.SemaphoreType.DMA((tiles, n_z)),
         pltpu.SemaphoreType.DMA((tiles,)),
+        pltpu.SemaphoreType.DMA((tiles,)),
+        pltpu.SemaphoreType.DMA((n_z,)),
+        pltpu.SemaphoreType.DMA((2,)),
     ]
     p_new, v_new, slip = pl.pallas_call(
         functools.partial(kernel, sizes),
@@ -546,11 +593,11 @@
             jax.ShapeDtypeStruct((3,) + box, F32),
             jax.ShapeDtypeStruct((1, per // n_z), F32),
         ],
-        in_specs=[hbm] * 4 + [vmem] * 6,
-        out_specs=[hbm, hbm, vmem],
+        in_specs=[hbm] * 10,
+        out_specs=[vmem] * 3,
         scratch_shapes=scratch,
         compiler_params=pltpu.CompilerParams(
-            collective_id=0, has_side_effects=True, vmem_limit_bytes=32 * 1024 * 1024
+            collective_id=0, has_side_effects=True, vmem_limit_bytes=64 * 1024 * 1024 - 64 * 1024
         ),
     )(
         pressure,

time: 34.4 us -> 28.8 us (0.84)
  local copies, waits for them, and re-layouts: 9.02 us -> 3.85 us
    unnamed x23 -> x5, local copies, waits for them, and re-layouts: 9.02 us -> 3.85 us
where the time goes in v2:
time: 28.8 us; the launch traced here: 28.6 us
  Pallas kernels  24.1 us (84%)
  local copies, waits for them, and re-layouts  3.85 us (13%)
  between operations  0.64 us (2%)
    pallas_call x1, Pallas kernels, local(): pl.pallas_call(functools.partial(kernel, sizes), out_shape=[jax.ShapeDtyp...  24.1 us
    unnamed x5, local copies, waits for them, and re-layouts  3.85 us

profile of v2, /device:TPU:0, one launch (start us, length us, event | category | flops | bytes accessed | tf_op | source)
XLA Modules:
  0.0 28.6 jit_solution(5556791489530385442)
XLA Ops:
  0.6 24.1 %shard_map.121 = (f32[16,16,128]{2,1,0:T(8,128)}, f32[3,16,16,128]{3,2,1,0:T(8,128)}, f32[1,32]{1,0:T(1,128)}) custom-call(f32[16,16,128]{2,1,0:T(8,128)} %p_in.1, f32[3,16,16,128]{3,2,1,0:T(8,128)} %v_in.1, f32[16,16,128]{2,1,0:T(8,128)} %d_in.1, f32[16,16,128]{2,1,0:T(8,128)} %b_in.1, f32[1,1,256]{2,1,0:T(1,128)} %weight_in.1, s32[1,1,256]{2,1,0:T(1,128)} %patch_in.1, ...), custom_call_target="tpu_custom_call" | custom-call | tf_op jit(solution)/shard_map/pallas_call | solution.py:589
  24.7 1.6 %copy.16 = f32[16,16,128]{2,1,0:T(8,128)} copy(f32[16,16,128]{2,1,0:T(8,128)} %get-tuple-element.12) | data formatting | bytes 262144
  26.3 0.0 copy-start
  26.3 1.8 %copy.17 = f32[3,16,16,128]{3,2,1,0:T(8,128)} copy(f32[3,16,16,128]{3,2,1,0:T(8,128)} %get-tuple-element.13) | data formatting | bytes 786432
  28.1 0.0 copy-done
  28.1 0.5 %copy.18 = f32[32]{0:T(128)} copy(f32[32]{0:T(128)S(1)} %bitcast.7) | data formatting | bytes 256
Async XLA Ops:
  26.3 1.8 %copy-start = (f32[1,32]{1,0:T(1,128)S(1)}, f32[1,32]{1,0:T(1,128)}, u32[]{:S(2)}) copy-start(f32[1,32]{1,0:T(1,128)} %get-tuple-element.8) | copy-start | bytes 388

commit v3 on v2

--- a/solution.py
+++ b/solution.py
@@ -530,6 +530,17 @@
                 depth_copy(c, my_slot).wait_send()
 
 
+def write_out(p_in, v_in, slip_in, p_out, v_out, slip_out, sem):
+    copies = [
+        pltpu.make_async_copy(src, dst, sem.at[n])
+        for n, (src, dst) in enumerate([(v_in, v_out), (p_in, p_out), (slip_in, slip_out)])
+    ]
+    for copy in copies:
+        copy.start()
+    for copy in copies:
+        copy.wait()
+
+
 def local(sizes, pressure, velocity, inv_density, bulk, node_weight, node_patch, patch_slot,
           gauge_x, gauge_y, gauge_misfit):
     rows_x, rows_y, depth = pressure.shape
@@ -586,18 +597,20 @@
         pltpu.SemaphoreType.DMA((n_z,)),
         pltpu.SemaphoreType.DMA((2,)),
     ]
+    colored = [pltpu.VMEM(box, F32), pltpu.VMEM((3,) + box, F32), pltpu.VMEM((1, per // n_z), F32)]
+    shapes = [
+        jax.ShapeDtypeStruct(box, F32),
+        jax.ShapeDtypeStruct((3,) + box, F32),
+        jax.ShapeDtypeStruct((1, per // n_z), F32),
+    ]
     p_new, v_new, slip = pl.pallas_call(
         functools.partial(kernel, sizes),
-        out_shape=[
-            jax.ShapeDtypeStruct(box, F32),
-            jax.ShapeDtypeStruct((3,) + box, F32),
-            jax.ShapeDtypeStruct((1, per // n_z), F32),
-        ],
+        out_shape=colored,
         in_specs=[hbm] * 10,
         out_specs=[vmem] * 3,
         scratch_shapes=scratch,
         compiler_params=pltpu.CompilerParams(
-            collective_id=0, has_side_effects=True, vmem_limit_bytes=64 * 1024 * 1024 - 64 * 1024
+            collective_id=0, has_side_effects=True, vmem_limit_bytes=64 * 1024 * 1024 - 1400 * 1024
         ),
     )(
         pressure,
@@ -611,6 +624,15 @@
         gauge_y.reshape(1, -1),
         gauge_misfit,
     )
+    anywhere = pl.BlockSpec(memory_space=pl.ANY)
+    p_new, v_new, slip = pl.pallas_call(
+        write_out,
+        out_shape=shapes,
+        in_specs=[anywhere] * 3,
+        out_specs=[anywhere] * 3,
+        scratch_shapes=[pltpu.SemaphoreType.DMA((3,))],
+        compiler_params=pltpu.CompilerParams(vmem_limit_bytes=2 * 1024 * 1024),
+    )(p_new, v_new, slip)
     return p_new, v_new, slip.reshape(per // n_z)
 
 

time: 28.8 us -> 24.9 us (0.86)
  local copies, waits for them, and re-layouts: 3.85 us -> 0 us
    unnamed x5 -> x0, local copies, waits for them, and re-layouts: 3.85 us -> none
    pallas_call x1 -> x2, Pallas kernels: 24.1 us -> 24.1 us  [the longest x1 23.3 us: local(): pl.pallas_call(functools.partial(kernel, sizes), out_shape=colored, in_sp...]
where the time goes in v3:
time: 24.9 us; the launch traced here: 24.8 us
  Pallas kernels  24.1 us (97%)
  between operations  0.64 us (3%)
    pallas_call x1, Pallas kernels, local(): pl.pallas_call(functools.partial(kernel, sizes), out_shape=colored, in_sp...  23.3 us
    pallas_call x1, Pallas kernels, local(): pl.pallas_call(write_out, out_shape=shapes, in_specs=[anywhere] * 3, out_...  0.82 us

profile of v3, /device:TPU:0, one launch (start us, length us, event | category | flops | bytes accessed | tf_op | source)
XLA Modules:
  0.0 24.8 jit_solution(12958772230633270481)
XLA Ops:
  0.6 23.3 %shard_map.121 = (f32[16,16,128]{2,1,0:T(8,128)S(1)}, f32[3,16,16,128]{3,2,1,0:T(8,128)S(1)}, f32[1,32]{1,0:T(1,128)S(1)}) custom-call(f32[16,16,128]{2,1,0:T(8,128)} %p_in.1, f32[3,16,16,128]{3,2,1,0:T(8,128)} %v_in.1, f32[16,16,128]{2,1,0:T(8,128)} %d_in.1, f32[16,16,128]{2,1,0:T(8,128)} %b_in.1, f32[1,1,256]{2,1,0:T(1,128)} %weight_in.1, ...), custom_call_target="tpu_custom_call" | custom-call | tf_op jit(solution)/shard_map/pallas_call | solution.py:606
  23.9 0.8 %shard_map.122 = (f32[16,16,128]{2,1,0:T(8,128)}, f32[3,16,16,128]{3,2,1,0:T(8,128)}, f32[1,32]{1,0:T(1,128)}) custom-call(f32[16,16,128]{2,1,0:T(8,128)S(1)} %get-tuple-element.9.p_in, f32[3,16,16,128]{3,2,1,0:T(8,128)S(1)} %get-tuple-element.10.v_in, f32[1,32]{1,0:T(1,128)S(1)} %get-tuple-element.11.slip_in), custom_call_target="tpu_custom_call" | custom-call | tf_op jit(solution)/shard_map/pallas_call | solution.py:628

commit v4 on v3

--- a/solution.py
+++ b/solution.py
@@ -12,7 +12,6 @@
 AXES = ("gx", "gy", "gz")
 YA = 8
 F32 = jnp.float32
-HIGHEST = lax.Precision.HIGHEST
 NT = (((1,), (1,)), ((), ()))
 
 
@@ -46,8 +45,9 @@
     bulk,
     pack_edge,
     vz_edge,
-    fill_p,
-    fill_v,
+    vy_edge,
+    vz_change,
+    bulk_pack,
     y_send,
     y_recv,
     z_send,
@@ -157,6 +157,12 @@
                 barrier, inc=1, device_id=(me[0], me[1], c), device_id_type=MESH_ID
             )
 
+    for y in (YA - 1, YA + rows_y):
+        zero = jnp.zeros((rows_x, 1, depth), F32)
+        vy[:, y : y + 1, :] = zero
+        for s in range(ITERS):
+            p_ext[s, 2 : rows_x + 2, y : y + 1, :] = zero
+
     for side in (0, 1):
 
         @pl.when(jnp.logical_not(has[0, side]))
@@ -187,12 +193,6 @@
             rolled = pltpu.roll(read(j // halves, (j % halves) * 8), (4 * j + 2) % depth, 1)
             q = jnp.where(group == j, rolled, q)
         return q
-
-    def unpack(tile_value, ref):
-        for j in range(rows_x * halves):
-            ref[j // halves, pl.ds((j % halves) * 8, 8), :] = pltpu.roll(
-                tile_value, (-(4 * j + 2)) % depth, 1
-            )
 
     def coefs(level):
         first = root * depth
@@ -207,6 +207,10 @@
     up, mid, low = coefs(me[2] * depth + row_lane)
     up_e, mid_e, low_e = coefs(
         jnp.where(quad == 1, me[2] * depth - 1, (me[2] + 1) * depth)
+    )
+
+    up_o, mid_o, low_o = coefs(
+        me[2] * depth + jnp.where(quad < 2, depth - 2 + quad, quad - 2)
     )
 
     def copy_x(s, side, to):
@@ -267,15 +271,21 @@
             return [init_copy(yi_send.at[side], yi_recv.at[1 - side], to, 2 + side, 3 - side)]
         return [init_copy(zi_send, zi_recv.at[1 - side], to, 4 + side, 5 - side)]
 
+    def start_faces(s, axis):
+        for f in faces:
+            if f[0] == axis:
+
+                @pl.when(has[f])
+                def _(f=f):
+                    step_copies[axis](s, f[1], other[f]).start()
+
     def send(s):
-        z_send[s] = packed(lambda x, y: p_ext[s, 2 + x, pl.ds(YA + y, 8), :])
+        start_faces(s, 0)
         y_send[s, 0] = p_ext[s, 2 : rows_x + 2, YA : YA + 2, :]
         y_send[s, 1] = p_ext[s, 2 : rows_x + 2, YA + rows_y - 2 : YA + rows_y, :]
-        for f in faces:
-
-            @pl.when(has[f])
-            def _(f=f):
-                step_copies[f[0]](s, f[1], other[f]).start()
+        start_faces(s, 1)
+        z_send[s] = packed(lambda x, y: p_ext[s, 2 + x, pl.ds(YA + y, 8), :])
+        start_faces(s, 2)
 
     def receive(s):
         for f in faces:
@@ -284,39 +294,43 @@
             def _(f=f):
                 step_copies[f[0]](s, 1 - f[1], other[f]).wait_recv()
 
-        p_ext[s, 2 : rows_x + 2, YA - 2 : YA, :] = y_recv[s, 0]
-        p_ext[s, 2 : rows_x + 2, YA + rows_y : YA + rows_y + 2, :] = y_recv[s, 1]
-
-    def update(s, last):
-        own = z_send[s]
-        halo = jnp.where(quad < 2, z_recv[s, 0], z_recv[s, 1])
-        above = pltpu.roll(jnp.where(quad == 2, own, halo), depth - 1, 1)
-        below = pltpu.roll(jnp.where(quad == 1, own, halo), 1, 1)
-        edge = vz_edge[...] - 0.5 * pack_edge[...] * (
-            up_e * above + mid_e * halo + low_e * below
-        )
-        vz_edge[...] = edge
-        unpack(halo, fill_p)
-        unpack(edge, fill_v)
-
-        def along_x(i, _):
-            at = pl.ds(i * 3, 3)
-            ahead = p_ext[s, pl.ds(i * 3 + 2, 3), y_in, :]
-            behind = p_ext[s, pl.ds(i * 3, 3), y_in, :]
-            vx[at] = vx[at] - 0.25 * inv[at] * (ahead - behind)
-            return 0
-
-        for i in range((rows_x + 2) // 3):
-            along_x(i, 0)
-        inner = slice(2, rows_x + 2)
-        vy[:, YA - 1 : YA, :] = vy[:, YA - 1 : YA, :] - 0.25 * inv_y[0] * (
-            p_ext[s, inner, YA : YA + 1, :] - p_ext[s, inner, YA - 2 : YA - 1, :]
-        )
-        end_y = YA + rows_y
-        vy[:, end_y : end_y + 1, :] = vy[:, end_y : end_y + 1, :] - 0.25 * inv_y[1] * (
-            p_ext[s, inner, end_y + 1 : end_y + 2, :] - p_ext[s, inner, end_y - 1 : end_y, :]
-        )
-        chunk = 4
+    def pressure_rows(s, x, n, last):
+        at = pl.ds(x, n)
+        w = vz[at]
+        above_v = pltpu.roll(jnp.where(row_lane == 0, 0.0, w), depth - 1, 2)
+        below_v = pltpu.roll(jnp.where(row_lane == depth - 1, 0.0, w), 1, 2)
+        spread = (
+            0.5 * (vx[pl.ds(x + 2, n)] - vx[at])
+            + 0.5 * (vy[at, pl.ds(YA + 1, rows_y), :] - vy[at, pl.ds(YA - 1, rows_y), :])
+            + (up * above_v + mid * w + low * below_v)
+        )
+        added = jnp.where(row_lane == 0, pltpu.roll(source[at], (depth - s) % depth, 2), 0.0)
+        new = p_ext[s, pl.ds(x + 2, n), y_in, :] - 0.5 * bulk[at] * spread + added
+        if last:
+            p_out[at] = new
+        else:
+            p_ext[s + 1, pl.ds(x + 2, n), y_in, :] = new
+
+    def velocity_x(s, at, n):
+        rows = pl.ds(at, n)
+        vx[rows] = vx[rows] - 0.25 * inv[rows] * (
+            p_ext[s, pl.ds(at + 2, n), y_in, :] - p_ext[s, rows, y_in, :]
+        )
+
+    near_edge = (lane < 2) | (lane >= depth - 2)
+
+    def add_packed(value, ref, x_at, y_at):
+        for j in range(rows_x * halves):
+            rolled = pltpu.roll(value, (-(4 * j + 2)) % depth, 1)
+            at = (x_at + j // halves, pl.ds(y_at + (j % halves) * 8, 8))
+            ref[at] = ref[at] + jnp.where(near_edge, rolled, 0.0)
+
+    chunk = 4
+
+    def inner(s, last):
+        half = (rows_x - 2) // 2
+        velocity_x(s, 2, half)
+        velocity_x(s, 2 + half, rows_x - 2 - half)
         for i in range(0, rows_x, chunk):
             at = pl.ds(i, chunk)
             at_p = pl.ds(i + 2, chunk)
@@ -325,45 +339,66 @@
             vy[at, y_in, :] = vy[at, y_in, :] - 0.25 * rho * (
                 p_ext[s, at_p, pl.ds(YA + 1, rows_y), :] - p_ext[s, at_p, pl.ds(YA - 1, rows_y), :]
             )
-            halo_p = fill_p[at]
-            above_p = pltpu.roll(jnp.where(row_lane == 0, halo_p, here), depth - 1, 2)
-            below_p = pltpu.roll(jnp.where(row_lane == depth - 1, halo_p, here), 1, 2)
+            above_p = pltpu.roll(jnp.where(row_lane == 0, 0.0, here), depth - 1, 2)
+            below_p = pltpu.roll(jnp.where(row_lane == depth - 1, 0.0, here), 1, 2)
             vz[at] = vz[at] - 0.5 * rho * (up * above_p + mid * here + low * below_p)
-        if last:
-            v_out[0] = vx[1 : rows_x + 1]
-            v_out[1] = vy[:, YA : YA + rows_y, :]
-            v_out[2] = vz[...]
-            owner_sums()
-        for i in range(0, rows_x, chunk):
-            at = pl.ds(i, chunk)
-            at_p = pl.ds(i + 2, chunk)
-            w = vz[at]
-            halo_v = fill_v[at]
-            above_v = pltpu.roll(jnp.where(row_lane == 0, halo_v, w), depth - 1, 2)
-            below_v = pltpu.roll(jnp.where(row_lane == depth - 1, halo_v, w), 1, 2)
-            spread = (
-                0.5 * (vx[pl.ds(i + 2, chunk)] - vx[at])
-                + 0.5 * (vy[at, pl.ds(YA + 1, rows_y), :] - vy[at, pl.ds(YA - 1, rows_y), :])
-                + (up * above_v + mid * w + low * below_v)
+        for i in range(2, rows_x - 2, chunk):
+            pressure_rows(s, i, chunk, last)
+
+    def outer(s, last):
+        velocity_x(s, 0, 2)
+        velocity_x(s, rows_x, 2)
+        pressure_rows(s, 0, 2, last)
+        pressure_rows(s, rows_x - 2, 2, last)
+
+        ref, x_at, y_at = (p_out, 0, 0) if last else (p_ext.at[s + 1], 2, YA)
+        rows = pl.ds(x_at, rows_x)
+        for side, edge, after, sign in ((0, 0, 1, 0.25), (1, rows_y - 1, rows_y - 2, -0.25)):
+            near = y_recv[s, side, :, 1 - side : 2 - side, :]
+            far = y_recv[s, side, :, side : side + 1, :]
+            halo_v = vy_edge[side] - sign * inv_y[side] * (
+                y_send[s, side, :, side : side + 1, :] - far
             )
-            added = jnp.where(row_lane == 0, pltpu.roll(source[at], (depth - s) % depth, 2), 0.0)
-            new = p_ext[s, at_p, y_in, :] - 0.5 * bulk[at] * spread + added
-            if last:
-                p_out[at] = new
-            else:
-                p_ext[s + 1, at_p, y_in, :] = new
-
-    for load in loads:
+            vy_edge[side] = halo_v
+            change = sign * inv[1 : rows_x + 1, edge : edge + 1, :] * near
+            at_v = (slice(None), slice(YA + edge, YA + edge + 1), slice(None))
+            vy[at_v] = vy[at_v] + change
+            at_edge = (rows, pl.ds(y_at + edge, 1))
+            ref[at_edge] = ref[at_edge] + sign * bulk[:, edge : edge + 1, :] * halo_v
+            at_after = (rows, pl.ds(y_at + after, 1))
+            ref[at_after] = ref[at_after] + sign * bulk[:, after : after + 1, :] * change
+
+        own = z_send[s]
+        halo = jnp.where(quad < 2, z_recv[s, 0], z_recv[s, 1])
+        above = pltpu.roll(jnp.where(quad == 2, own, halo), depth - 1, 1)
+        below = pltpu.roll(jnp.where(quad == 1, own, halo), 1, 1)
+        edge = vz_edge[...] - 0.5 * pack_edge[...] * (
+            up_e * above + mid_e * halo + low_e * below
+        )
+        vz_edge[...] = edge
+        change = -0.5 * zi_send[1] * jnp.where(
+            quad == 1,
+            up_o * pltpu.roll(halo, depth - 1, 1),
+            jnp.where(quad == 2, low_o * pltpu.roll(halo, 1, 1), 0.0),
+        )
+        vz_change[...] = change
+        ahead = pltpu.roll(jnp.where(quad == 2, edge, change), depth - 1, 1)
+        behind = pltpu.roll(jnp.where(quad == 1, edge, change), 1, 1)
+        spread = jnp.where(quad < 2, up_o * ahead, low_o * behind) + mid_o * change
+        add_packed(-0.5 * bulk_pack[...] * spread, ref, x_at, y_at)
+
+    count = sum(has[f].astype(jnp.int32) for f in faces)
+    count = count + jnp.where(at_sea, tiles - 1 + n_z - 1, 0)
+    loads[0].wait()
+    pl.semaphore_wait(barrier, count)
+    send(0)
+    for load in loads[1:]:
         load.wait()
     zi_send[0] = packed(lambda x, y: vz[x, pl.ds(y, 8), :])
     zi_send[1] = packed(lambda x, y: inv[1 + x, pl.ds(y, 8), :])
     for side, y in ((0, 0), (1, rows_y - 1)):
         yi_send[side, :, 0:1, :] = vy[:, YA + y : YA + y + 1, :]
         yi_send[side, :, 1:2, :] = inv[1 : rows_x + 1, y : y + 1, :]
-    count = sum(has[f].astype(jnp.int32) for f in faces)
-    count = count + jnp.where(at_sea, tiles - 1 + n_z - 1, 0)
-    pl.semaphore_wait(barrier, count)
-    send(0)
     for f in faces:
 
         @pl.when(has[f])
@@ -376,11 +411,30 @@
     inside = (cell_x >= 0) & (cell_x < rows_x) & (cell_y >= 0) & (cell_y < rows_y)
     cell = jnp.where(inside, cell_x * rows_y + cell_y, -1)
     gauges = cell.shape[1]
-    hot = (lax.broadcasted_iota(jnp.int32, (cells, gauges), 0) == cell).astype(F32)
-    scaled = misfit_ref[...] * jnp.where(me[2] == 0, 0.5, 0.0).astype(F32)
-    scaled = jnp.concatenate([scaled, jnp.zeros((depth - ITERS, gauges), F32)], axis=0)
-    planes = lax.dot_general(hot, scaled, NT, precision=HIGHEST, preferred_element_type=F32)
-    source[...] = planes.reshape(rows_x, rows_y, depth)
+
+    def three_parts(value):
+        high = value.astype(jnp.bfloat16).astype(F32)
+        rest = value - high
+        middle = rest.astype(jnp.bfloat16).astype(F32)
+        return high, middle, rest - middle
+
+    @pl.when(me[2] != 0)
+    def _():
+        source[...] = jnp.zeros_like(source)
+
+    @pl.when(me[2] == 0)
+    def _():
+        hot = lax.broadcasted_iota(jnp.int32, (cells, gauges), 0) == cell
+        hot = hot.astype(F32).astype(jnp.bfloat16)
+        scaled = jnp.concatenate(
+            [0.5 * misfit_ref[...], jnp.zeros((depth - ITERS, gauges), F32)], axis=0
+        )
+        planes = jnp.zeros((cells, depth), F32)
+        for value in three_parts(scaled):
+            planes = planes + lax.dot_general(
+                hot, value.astype(jnp.bfloat16), NT, preferred_element_type=F32
+            )
+        source[...] = planes.reshape(rows_x, rows_y, depth)
 
     nodes = patch_ref.shape[-1]
     patches = slot_ref.shape[1]
@@ -388,26 +442,28 @@
     shift = per.bit_length() - 1
     assert per == 1 << shift and per == 128
     block = min(patches, 1024)
-    patch = patch_ref[...].reshape(1, nodes)
-    slot_parts = jnp.zeros((8, nodes), F32)
-    first_row = lax.broadcasted_iota(jnp.int32, (8, block), 0) == 0
-    for at in range(0, patches, block):
-        slots = slot_ref[:, at : at + block]
-        table = jnp.where(first_row, slots >> shift, slots & (per - 1)).astype(F32)
-        hot = lax.broadcasted_iota(jnp.int32, (block, nodes), 0) + at == patch
-        slot_parts = slot_parts + jnp.dot(
-            table.astype(jnp.bfloat16),
-            hot.astype(F32).astype(jnp.bfloat16),
-            preferred_element_type=F32,
-        )
-    slot = (slot_parts[0:1] * per + slot_parts[1:2]).astype(jnp.int32)
-    for at in range(0, patches, block):
-        hot = lax.broadcasted_iota(jnp.int32, (block, nodes), 0) + at == slot
-        slot_hot[pl.ds(at, block), :] = hot.astype(F32).astype(jnp.bfloat16)
-    node = lax.broadcasted_iota(jnp.int32, (depth, nodes), 1)
-    spread_hot[...] = (
-        lax.broadcasted_iota(jnp.int32, (depth, nodes), 0) == 4 * (node >> 3) + 2
-    ).astype(F32)
+
+    def slot_tables():
+        patch = patch_ref[...].reshape(1, nodes)
+        slot_parts = jnp.zeros((8, nodes), F32)
+        first_row = lax.broadcasted_iota(jnp.int32, (8, block), 0) == 0
+        for at in range(0, patches, block):
+            slots = slot_ref[:, at : at + block]
+            table = jnp.where(first_row, slots >> shift, slots & (per - 1)).astype(F32)
+            hot = lax.broadcasted_iota(jnp.int32, (block, nodes), 0) + at == patch
+            slot_parts = slot_parts + jnp.dot(
+                table.astype(jnp.bfloat16),
+                hot.astype(F32).astype(jnp.bfloat16),
+                preferred_element_type=F32,
+            )
+        slot = (slot_parts[0:1] * per + slot_parts[1:2]).astype(jnp.int32)
+        for at in range(0, patches, block):
+            hot = lax.broadcasted_iota(jnp.int32, (block, nodes), 0) + at == slot
+            slot_hot[pl.ds(at, block), :] = hot.astype(F32).astype(jnp.bfloat16)
+        node = lax.broadcasted_iota(jnp.int32, (depth, nodes), 1)
+        spread_hot[...] = (
+            lax.broadcasted_iota(jnp.int32, (depth, nodes), 0) == 4 * (node >> 3) + 2
+        ).astype(F32).astype(jnp.bfloat16)
 
     def slip_copy(o_x, o_y, source_tile):
         return pltpu.make_async_remote_copy(
@@ -435,15 +491,17 @@
         @pl.when(at_sea)
         def _():
             mine = 0.5 * jnp.where(me[2] == root, sea, pltpu.roll(sea, 1, 1))
-            values = jnp.dot(mine, spread_hot[...], precision=HIGHEST, preferred_element_type=F32)
+            values = jnp.dot(
+                jnp.concatenate(three_parts(mine), axis=0).astype(jnp.bfloat16),
+                spread_hot[...],
+                preferred_element_type=F32,
+            )
+            values = values[0:8] + values[8:16] + values[16:24]
             sub = lax.broadcasted_iota(jnp.int32, (8, nodes), 0)
             col = lax.broadcasted_iota(jnp.int32, (8, nodes), 1)
             row = jnp.sum(jnp.where((col & 7) == sub, values, 0.0), axis=0, keepdims=True)
             row = row * weight_ref[...].reshape(1, nodes)
-            high = row.astype(jnp.bfloat16).astype(F32)
-            rest = row - high
-            middle = rest.astype(jnp.bfloat16).astype(F32)
-            lowest = rest - middle
+            high, middle, lowest = three_parts(row)
             split = jnp.where(
                 sub == 0, high, jnp.where(sub == 1, middle, jnp.where(sub == 2, lowest, 0.0))
             ).astype(jnp.bfloat16)
@@ -469,34 +527,49 @@
                 def _(c=c):
                     depth_copy(c, my_slot).start()
 
-    for f in faces:
-
-        @pl.when(has[f])
-        def _(f=f):
-            for copy in init_copies(f[0], 1 - f[1], other[f]):
-                copy.wait_recv()
-
-    for side, y in ((0, YA - 1), (1, YA + rows_y)):
-        vy[:, y : y + 1, :] = yi_recv[side, :, 0:1, :]
-        inv_y[side] = yi_recv[side, :, 1:2, :]
-    kept = (quad == 1) | (quad == 2)
-    vz_edge[...] = jnp.where(
-        kept, jnp.where(quad == 1, zi_recv[0, 0], zi_recv[1, 0]), 0.0
-    )
-    pack_edge[...] = jnp.where(
-        kept, jnp.where(quad == 1, zi_recv[0, 1], zi_recv[1, 1]), 0.0
-    )
-
-    receive(0)
+    bulk_pack[...] = packed(lambda x, y: bulk[x, pl.ds(y, 8), :])
+
+    def receive_start():
+        for f in faces:
+
+            @pl.when(has[f])
+            def _(f=f):
+                for copy in init_copies(f[0], 1 - f[1], other[f]):
+                    copy.wait_recv()
+
+        for side in (0, 1):
+            vy_edge[side] = yi_recv[side, :, 0:1, :]
+            inv_y[side] = yi_recv[side, :, 1:2, :]
+        kept = (quad == 1) | (quad == 2)
+        vz_edge[...] = jnp.where(
+            kept, jnp.where(quad == 1, zi_recv[0, 0], zi_recv[1, 0]), 0.0
+        )
+        pack_edge[...] = jnp.where(
+            kept, jnp.where(quad == 1, zi_recv[0, 1], zi_recv[1, 1]), 0.0
+        )
+
     sea = z_send[0]
-    update(0, False)
-    for s in range(1, ITERS):
-        send(s)
-        sea = sea + z_send[s]
-        if s == ITERS - 1:
-            finish_sea(sea)
+    for s in range(ITERS):
+        last = s == ITERS - 1
+        if s > 0:
+            send(s)
+            sea = sea + z_send[s]
+            if last:
+                finish_sea(sea)
+            add_packed(vz_change[...], vz, 0, 0)
+        inner(s, last)
+        if s == 1:
+            pl.when(at_sea)(slot_tables)
         receive(s)
-        update(s, s == ITERS - 1)
+        if s == 0:
+            receive_start()
+        if last:
+            owner_sums()
+        outer(s, last)
+    add_packed(vz_change[...], vz, 0, 0)
+    v_out[0] = vx[1 : rows_x + 1]
+    v_out[1] = vy[:, YA : YA + rows_y, :]
+    v_out[2] = vz[...]
 
     for slot_at, c in ((0, root - 1), (1, root)):
 
@@ -570,8 +643,9 @@
         pltpu.VMEM(box, F32),
         pltpu.VMEM((8, depth), F32),
         pltpu.VMEM((8, depth), F32),
-        pltpu.VMEM(box, F32),
-        pltpu.VMEM(box, F32),
+        pltpu.VMEM((2, rows_x, 1, depth), F32),
+        pltpu.VMEM((8, depth), F32),
+        pltpu.VMEM((8, depth), F32),
         pltpu.VMEM((ITERS, 2, rows_x, 2, depth), F32),
         pltpu.VMEM((ITERS, 2, rows_x, 2, depth), F32),
         pltpu.VMEM((ITERS, 8, depth), F32),
@@ -582,7 +656,7 @@
         pltpu.VMEM((2, 2, 8, depth), F32),
         pltpu.VMEM(box, F32),
         pltpu.VMEM((patches, nodes), jnp.bfloat16),
-        pltpu.VMEM((depth, nodes), F32),
+        pltpu.VMEM((depth, nodes), jnp.bfloat16),
         pltpu.VMEM((tiles, 1, per), F32),
         pltpu.VMEM((tiles, 1, per), F32),
         pltpu.VMEM((1, per), F32),

time: 24.9 us -> 24.5 us (0.984)
  Pallas kernels: 24.1 us -> 23.7 us
    pallas_call x1, Pallas kernels: 23.3 us -> 22.9 us  [local(): pl.pallas_call(functools.partial(kernel, sizes), out_shape=colored, in_sp...]
where the time goes in v4:
time: 24.5 us; the launch traced here: 24.4 us
  Pallas kernels  23.7 us (97%)
  between operations  0.64 us (3%)
    pallas_call x1, Pallas kernels, local(): pl.pallas_call(functools.partial(kernel, sizes), out_shape=colored, in_sp...  22.9 us
    pallas_call x1, Pallas kernels, local(): pl.pallas_call(write_out, out_shape=shapes, in_specs=[anywhere] * 3, out_...  0.82 us

profile of v4, /device:TPU:0, one launch (start us, length us, event | category | flops | bytes accessed | tf_op | source)
XLA Modules:
  0.0 24.4 jit_solution(5225612270048530412)
XLA Ops:
  0.6 22.9 %shard_map.121 = (f32[16,16,128]{2,1,0:T(8,128)S(1)}, f32[3,16,16,128]{3,2,1,0:T(8,128)S(1)}, f32[1,32]{1,0:T(1,128)S(1)}) custom-call(f32[16,16,128]{2,1,0:T(8,128)} %p_in.1, f32[3,16,16,128]{3,2,1,0:T(8,128)} %v_in.1, f32[16,16,128]{2,1,0:T(8,128)} %d_in.1, f32[16,16,128]{2,1,0:T(8,128)} %b_in.1, f32[1,1,256]{2,1,0:T(1,128)} %weight_in.1, ...), custom_call_target="tpu_custom_call" | custom-call | tf_op jit(solution)/shard_map/pallas_call | solution.py:680
  23.6 0.8 %shard_map.122 = (f32[16,16,128]{2,1,0:T(8,128)}, f32[3,16,16,128]{3,2,1,0:T(8,128)}, f32[1,32]{1,0:T(1,128)}) custom-call(f32[16,16,128]{2,1,0:T(8,128)S(1)} %get-tuple-element.9.p_in, f32[3,16,16,128]{3,2,1,0:T(8,128)S(1)} %get-tuple-element.10.v_in, f32[1,32]{1,0:T(1,128)S(1)} %get-tuple-element.11.slip_in), custom_call_target="tpu_custom_call" | custom-call | tf_op jit(solution)/shard_map/pallas_call | solution.py:702

commit v5 on v4

--- a/solution.py
+++ b/solution.py
@@ -294,7 +294,7 @@
             def _(f=f):
                 step_copies[f[0]](s, 1 - f[1], other[f]).wait_recv()
 
-    def pressure_rows(s, x, n, last):
+    def pressure_rows(s, x, n):
         at = pl.ds(x, n)
         w = vz[at]
         above_v = pltpu.roll(jnp.where(row_lane == 0, 0.0, w), depth - 1, 2)
@@ -306,10 +306,7 @@
         )
         added = jnp.where(row_lane == 0, pltpu.roll(source[at], (depth - s) % depth, 2), 0.0)
         new = p_ext[s, pl.ds(x + 2, n), y_in, :] - 0.5 * bulk[at] * spread + added
-        if last:
-            p_out[at] = new
-        else:
-            p_ext[s + 1, pl.ds(x + 2, n), y_in, :] = new
+        p_ext[s + 1, pl.ds(x + 2, n), y_in, :] = new
 
     def velocity_x(s, at, n):
         rows = pl.ds(at, n)
@@ -327,7 +324,7 @@
 
     chunk = 4
 
-    def inner(s, last):
+    def inner(s):
         half = (rows_x - 2) // 2
         velocity_x(s, 2, half)
         velocity_x(s, 2 + half, rows_x - 2 - half)
@@ -343,15 +340,15 @@
             below_p = pltpu.roll(jnp.where(row_lane == depth - 1, 0.0, here), 1, 2)
             vz[at] = vz[at] - 0.5 * rho * (up * above_p + mid * here + low * below_p)
         for i in range(2, rows_x - 2, chunk):
-            pressure_rows(s, i, chunk, last)
-
-    def outer(s, last):
+            pressure_rows(s, i, chunk)
+
+    def outer(s):
         velocity_x(s, 0, 2)
         velocity_x(s, rows_x, 2)
-        pressure_rows(s, 0, 2, last)
-        pressure_rows(s, rows_x - 2, 2, last)
-
-        ref, x_at, y_at = (p_out, 0, 0) if last else (p_ext.at[s + 1], 2, YA)
+        pressure_rows(s, 0, 2)
+        pressure_rows(s, rows_x - 2, 2)
+
+        ref, x_at, y_at = p_ext.at[s + 1], 2, YA
         rows = pl.ds(x_at, rows_x)
         for side, edge, after, sign in ((0, 0, 1, 0.25), (1, rows_y - 1, rows_y - 2, -0.25)):
             near = y_recv[s, side, :, 1 - side : 2 - side, :]
@@ -548,24 +545,31 @@
             kept, jnp.where(quad == 1, zi_recv[0, 1], zi_recv[1, 1]), 0.0
         )
 
-    sea = z_send[0]
-    for s in range(ITERS):
+    vz_change[...] = jnp.zeros_like(vz_change)
+
+    def step(s, sea):
+        @pl.when(s > 0)
+        def _():
+            send(s)
+
+        sea = sea + z_send[s]
         last = s == ITERS - 1
-        if s > 0:
-            send(s)
-            sea = sea + z_send[s]
-            if last:
-                finish_sea(sea)
-            add_packed(vz_change[...], vz, 0, 0)
-        inner(s, last)
-        if s == 1:
-            pl.when(at_sea)(slot_tables)
+
+        @pl.when(last)
+        def _():
+            finish_sea(sea)
+
+        add_packed(vz_change[...], vz, 0, 0)
+        inner(s)
+        pl.when(at_sea & (s == 1))(slot_tables)
         receive(s)
-        if s == 0:
-            receive_start()
-        if last:
-            owner_sums()
-        outer(s, last)
+        pl.when(s == 0)(receive_start)
+        pl.when(last)(owner_sums)
+        outer(s)
+        return sea
+
+    lax.fori_loop(0, ITERS, step, jnp.zeros((8, depth), F32))
+    p_out[...] = p_ext[ITERS, 2 : rows_x + 2, YA : YA + rows_y, :]
     add_packed(vz_change[...], vz, 0, 0)
     v_out[0] = vx[1 : rows_x + 1]
     v_out[1] = vy[:, YA : YA + rows_y, :]
@@ -634,7 +638,7 @@
         pltpu.VMEM((1, gauges), jnp.int32),
         pltpu.VMEM((1, gauges), jnp.int32),
         pltpu.VMEM((ITERS, gauges), F32),
-        pltpu.VMEM((ITERS, rows_x + 4, wide_y, depth), F32),
+        pltpu.VMEM((ITERS + 1, rows_x + 4, wide_y, depth), F32),
         pltpu.VMEM((rows_x + 2, rows_y, depth), F32),
         pltpu.VMEM((rows_x, wide_y, depth), F32),
         pltpu.VMEM(box, F32),

time: 24.5 us -> 24.5 us (level)
  no operation moved by 1% of the time
where the time goes in v5:
time: 24.5 us; the launch traced here: 24.4 us
  Pallas kernels  23.7 us (97%)
  between operations  0.64 us (3%)
    pallas_call x1, Pallas kernels, local(): pl.pallas_call(functools.partial(kernel, sizes), out_shape=colored, in_sp...  22.9 us
    pallas_call x1, Pallas kernels, local(): pl.pallas_call(write_out, out_shape=shapes, in_specs=[anywhere] * 3, out_...  0.82 us

profile of v5, /device:TPU:0, one launch (start us, length us, event | category | flops | bytes accessed | tf_op | source)
XLA Modules:
  0.0 24.4 jit_solution(9985730960990352361)
XLA Ops:
  0.6 22.9 %shard_map.121 = (f32[16,16,128]{2,1,0:T(8,128)S(1)}, f32[3,16,16,128]{3,2,1,0:T(8,128)S(1)}, f32[1,32]{1,0:T(1,128)S(1)}) custom-call(f32[16,16,128]{2,1,0:T(8,128)} %p_in.1, f32[3,16,16,128]{3,2,1,0:T(8,128)} %v_in.1, f32[16,16,128]{2,1,0:T(8,128)} %d_in.1, f32[16,16,128]{2,1,0:T(8,128)} %b_in.1, f32[1,1,256]{2,1,0:T(1,128)} %weight_in.1, ...), custom_call_target="tpu_custom_call" | custom-call | tf_op jit(solution)/shard_map/pallas_call | solution.py:684
  23.6 0.8 %shard_map.122 = (f32[16,16,128]{2,1,0:T(8,128)}, f32[3,16,16,128]{3,2,1,0:T(8,128)}, f32[1,32]{1,0:T(1,128)}) custom-call(f32[16,16,128]{2,1,0:T(8,128)S(1)} %get-tuple-element.9.p_in, f32[3,16,16,128]{3,2,1,0:T(8,128)S(1)} %get-tuple-element.10.v_in, f32[1,32]{1,0:T(1,128)S(1)} %get-tuple-element.11.slip_in), custom_call_target="tpu_custom_call" | custom-call | tf_op jit(solution)/shard_map/pallas_call | solution.py:706

commit v6 on v4

--- a/solution.py
+++ b/solution.py
@@ -279,13 +279,19 @@
                 def _(f=f):
                     step_copies[axis](s, f[1], other[f]).start()
 
-    def send(s):
+    def send_x_y(s):
         start_faces(s, 0)
         y_send[s, 0] = p_ext[s, 2 : rows_x + 2, YA : YA + 2, :]
         y_send[s, 1] = p_ext[s, 2 : rows_x + 2, YA + rows_y - 2 : YA + rows_y, :]
         start_faces(s, 1)
+
+    def send_z(s):
         z_send[s] = packed(lambda x, y: p_ext[s, 2 + x, pl.ds(YA + y, 8), :])
         start_faces(s, 2)
+
+    def send(s):
+        send_x_y(s)
+        send_z(s)
 
     def receive(s):
         for f in faces:
@@ -552,10 +558,13 @@
     for s in range(ITERS):
         last = s == ITERS - 1
         if s > 0:
-            send(s)
-            sea = sea + z_send[s]
             if last:
-                finish_sea(sea)
+                send_z(s)
+                finish_sea(sea + z_send[s])
+                send_x_y(s)
+            else:
+                send(s)
+                sea = sea + z_send[s]
             add_packed(vz_change[...], vz, 0, 0)
         inner(s, last)
         if s == 1:

time: 24.5 us -> 24.5 us (level)
  no operation moved by 1% of the time
where the time goes in v6:
time: 24.5 us; the launch traced here: 24.3 us
  Pallas kernels  23.7 us (97%)
  between operations  0.64 us (3%)
    pallas_call x1, Pallas kernels, local(): pl.pallas_call(functools.partial(kernel, sizes), out_shape=colored, in_sp...  22.9 us
    pallas_call x1, Pallas kernels, local(): pl.pallas_call(write_out, out_shape=shapes, in_specs=[anywhere] * 3, out_...  0.82 us

profile of v6, /device:TPU:0, one launch (start us, length us, event | category | flops | bytes accessed | tf_op | source)
XLA Modules:
  0.0 24.3 jit_solution(10112512888951152097)
XLA Ops:
  0.6 22.9 %shard_map.121 = (f32[16,16,128]{2,1,0:T(8,128)S(1)}, f32[3,16,16,128]{3,2,1,0:T(8,128)S(1)}, f32[1,32]{1,0:T(1,128)S(1)}) custom-call(f32[16,16,128]{2,1,0:T(8,128)} %p_in.1, f32[3,16,16,128]{3,2,1,0:T(8,128)} %v_in.1, f32[16,16,128]{2,1,0:T(8,128)} %d_in.1, f32[16,16,128]{2,1,0:T(8,128)} %b_in.1, f32[1,1,256]{2,1,0:T(1,128)} %weight_in.1, ...), custom_call_target="tpu_custom_call" | custom-call | tf_op jit(solution)/shard_map/pallas_call | solution.py:689
  23.5 0.8 %shard_map.122 = (f32[16,16,128]{2,1,0:T(8,128)}, f32[3,16,16,128]{3,2,1,0:T(8,128)}, f32[1,32]{1,0:T(1,128)}) custom-call(f32[16,16,128]{2,1,0:T(8,128)S(1)} %get-tuple-element.9.p_in, f32[3,16,16,128]{3,2,1,0:T(8,128)S(1)} %get-tuple-element.10.v_in, f32[1,32]{1,0:T(1,128)S(1)} %get-tuple-element.11.slip_in), custom_call_target="tpu_custom_call" | custom-call | tf_op jit(solution)/shard_map/pallas_call | solution.py:711
